TPU v7x, 256 devices: a whole 4x4x8 slice. The times are simulated.
256 devices in a mesh: tm: 16 (over y_lo, z), rows: 16 (over x, y_hi, core).
Axes of the slice: x: 4, y: 4 (y_hi: 2, y_lo: 2; y = y_hi * 2 + y_lo), z: 8, core: 2. Of those that a mesh axis runs over, the one named last changes fastest.
Arguments:
- queries: bfloat16 [16, 128, 16, 3072], P('tm', 'rows'), may hold values from -6 to 6
- key_states: bfloat16 [16, 128, 16, 3072], P('tm', 'rows'), may hold values from -6 to 6
- value_states: bfloat16 [16, 128, 16, 3072], P('tm', 'rows'), may hold values from -12 to 12
- out_grad: bfloat16 [16, 128, 16, 3072], P('tm', 'rows'), may hold values from -6 to 6
Outputs:
- temporal_out: bfloat16 [16, 128, 16, 3072], P('tm', 'rows')
- query_grad: bfloat16 [16, 128, 16, 3072], P('tm', 'rows')
- key_grad: bfloat16 [16, 128, 16, 3072], P('tm', 'rows')
- value_grad: bfloat16 [16, 128, 16, 3072], P('tm', 'rows')
All inputs are finite; a program needn't handle non-finite values.
Results may differ from a plain program's by a relative error of at most 0.02.
Values may be sent and summed in bfloat16 or wider, within the bound.
No kernel may reach another device: no remote copies, remote signals or barrier semaphores. Data moves between devices by JAX's collectives and lax.ppermute only.
A program may use at most 128 MiB of HBM per device.

v0:
```python
import functools

import jax
import jax.numpy as jnp
from jax import lax
from jax.experimental import pallas as pl
from jax.experimental.pallas import tpu as pltpu
from jax.sharding import PartitionSpec as P

HEADS = 24
HEAD_DIM = 128
RADIUS = 3
SCALING = HEAD_DIM ** (-0.5)
NEG_FILL = -1e30
BF16 = jnp.bfloat16
F32 = jnp.float32

FWD_HEADS = 4
SCORE_HEADS = 4
TIME_HEADS = 4
BWD_HEADS = 4
RIM_HEADS = 8
LAST_HEADS = 6

NT = (((1,), (1,)), ((), ()))
NN = (((1,), (0,)), ((), ()))
TN = (((0,), (0,)), ((), ()))


def dot(left, right, dims):
    return lax.dot_general(left, right, dims, preferred_element_type=F32)


def lanes(head):
    return slice(head * HEAD_DIM, (head + 1) * HEAD_DIM)


def flat_rows(chunks):
    wide = chunks.astype(F32)
    return wide.reshape(wide.shape[0] * wide.shape[1], wide.shape[2])


def chunked(matrix, chunks):
    return matrix.reshape(chunks, matrix.shape[0] // chunks, matrix.shape[1])


def softmax_columns(scores):
    peak = jnp.max(scores, 0, keepdims=True)
    grown = jnp.exp((scores - peak) * SCALING)
    return grown * (1.0 / jnp.sum(grown, 0, keepdims=True))


def call(kernel, grid, in_specs, out_specs, out_shape, **more):
    return pl.pallas_call(
        kernel,
        grid=(grid,),
        in_specs=in_specs,
        out_specs=out_specs,
        out_shape=out_shape,
        compiler_params=pltpu.CompilerParams(vmem_limit_bytes=48 * 1024 * 1024),
        **more,
    )


def window_mask(first_row, total_rows, breadth, keys, queries):
    key = lax.broadcasted_iota(jnp.int32, (keys, queries), 0)
    query = lax.broadcasted_iota(jnp.int32, (keys, queries), 1)
    row_step = key // breadth - RADIUS - query // breadth
    col_step = key % breadth - query % breadth
    key_row = first_row - RADIUS + key // breadth
    return (
        (jnp.abs(row_step) <= RADIUS)
        & (jnp.abs(col_step) <= RADIUS)
        & (key_row >= 0)
        & (key_row < total_rows)
    )


def window_of(own_ref, low_ref, high_ref, half, head):
    rim = low_ref.shape[0] // 2
    rows = slice(half * rim, (half + 1) * rim)
    return jnp.concatenate(
        [low_ref[rows, lanes(head)], own_ref[:, lanes(head)], high_ref[rows, lanes(head)]], 0
    )


def spatial_fwd_kernel(total_rows, breadth, first_ref, q_ref, k_ref, v_ref, low_ref, high_ref, s_ref):
    queries = q_ref.shape[0]
    keys = queries + low_ref.shape[0]
    allowed = window_mask(first_ref[0], total_rows, breadth, keys, queries)
    for head in range(q_ref.shape[1] // HEAD_DIM):
        key = window_of(k_ref, low_ref, high_ref, 0, head)
        value = window_of(v_ref, low_ref, high_ref, 1, head)
        scores = jnp.where(allowed, dot(key, q_ref[:, lanes(head)], NT), NEG_FILL)
        weights = softmax_columns(scores).astype(BF16)
        s_ref[:, :, lanes(head)] = chunked(dot(weights, value, TN), s_ref.shape[0]).astype(BF16)


def spatial_bwd_kernel(
    total_rows, breadth, first_ref, q_ref, k_ref, v_ref, low_ref, high_ref, g_ref,
    qs_ref, ks_ref, vs_ref, to_low_ref, to_high_ref,
):
    queries = q_ref.shape[0]
    rim = low_ref.shape[0] // 2
    keys = queries + 2 * rim
    allowed = window_mask(first_ref[0], total_rows, breadth, keys, queries)
    for head in range(q_ref.shape[1] // HEAD_DIM):
        at = lanes(head)
        query = q_ref[:, at]
        key = window_of(k_ref, low_ref, high_ref, 0, head)
        value = window_of(v_ref, low_ref, high_ref, 1, head)
        grad = flat_rows(g_ref[:, :, at]).astype(BF16)
        probs = softmax_columns(jnp.where(allowed, dot(key, query, NT), NEG_FILL))
        weights = probs.astype(BF16)
        prob_grad = dot(value, grad, NT)
        grad_dot = jnp.sum(weights.astype(F32) * prob_grad, 0, keepdims=True)
        score_grad = (probs * (prob_grad - grad_dot)).astype(BF16)
        qs_ref[:, at] = dot(score_grad, key, TN) * SCALING
        key_wide = dot(score_grad, query, NN) * SCALING
        value_wide = dot(weights, grad, NN)
        ks_ref[:, at] = key_wide[rim : rim + queries]
        vs_ref[:, at] = value_wide[rim : rim + queries]
        to_low_ref[:rim, at] = key_wide[:rim].astype(BF16)
        to_low_ref[rim:, at] = value_wide[:rim].astype(BF16)
        to_high_ref[:rim, at] = key_wide[rim + queries :].astype(BF16)
        to_high_ref[rim:, at] = value_wide[rim + queries :].astype(BF16)


def same_position(rows, spots):
    left = lax.broadcasted_iota(jnp.int32, (rows, rows), 0)
    right = lax.broadcasted_iota(jnp.int32, (rows, rows), 1)
    return left % spots == right % spots


def temporal_scores_kernel(q_ref, k_ref, g_ref, sent_ref, grad_ref, probs_ref):
    del sent_ref
    frames, spots = q_ref.shape[0], q_ref.shape[1]
    same = same_position(frames * spots, spots)
    for head in range(q_ref.shape[2] // HEAD_DIM):
        at = lanes(head)
        query = flat_rows(q_ref[:, :, at]).astype(BF16)
        key = flat_rows(k_ref[:, :, at]).astype(BF16)
        grad = flat_rows(g_ref[:, :, at]).astype(BF16)
        probs = softmax_columns(jnp.where(same, dot(key, query, NT), NEG_FILL))
        probs_ref[head] = probs
        grad_ref[:, :, at] = chunked(dot(probs.astype(BF16), grad, NN), frames).astype(BF16)


def temporal_grads_kernel(q_ref, k_ref, g_ref, s_ref, probs_ref, out_ref):
    frames = q_ref.shape[0]
    width = q_ref.shape[2]
    for head in range(width // HEAD_DIM):
        at = lanes(head)
        query = flat_rows(q_ref[:, :, at]).astype(BF16)
        key = flat_rows(k_ref[:, :, at]).astype(BF16)
        grad = flat_rows(g_ref[:, :, at]).astype(BF16)
        spatial = flat_rows(s_ref[:, :, at]).astype(BF16)
        probs = probs_ref[head]
        weights = probs.astype(BF16)
        prob_grad = dot(spatial, grad, NT)
        grad_dot = jnp.sum(weights.astype(F32) * prob_grad, 0, keepdims=True)
        score_grad = (probs * (prob_grad - grad_dot)).astype(BF16)
        time_out = dot(weights, spatial, TN)
        query_part = dot(score_grad, key, TN) * SCALING
        key_part = dot(score_grad, query, NN) * SCALING
        for place, part in enumerate((time_out, query_part, key_part)):
            first = place * width + head * HEAD_DIM
            out_ref[:, :, first : first + HEAD_DIM] = chunked(part, frames).astype(BF16)


def rim_add_kernel(ks_ref, vs_ref, from_low_ref, from_high_ref, key_ref, value_ref):
    rim = from_low_ref.shape[0] // 2
    rows = ks_ref.shape[0]
    for sum_ref, out_ref, half in ((ks_ref, key_ref, 0), (vs_ref, value_ref, 1)):
        part = slice(half * rim, (half + 1) * rim)
        out_ref[:rim] = (sum_ref[:rim] + from_low_ref[part].astype(F32)).astype(out_ref.dtype)
        out_ref[rim : rows - rim] = sum_ref[rim : rows - rim].astype(out_ref.dtype)
        out_ref[rows - rim :] = (sum_ref[rows - rim :] + from_high_ref[part].astype(F32)).astype(
            out_ref.dtype
        )


def last_sum_kernel(back_ref, qs_ref, ks_ref, out_ref, query_ref, key_ref):
    for piece in range(back_ref.shape[2] // (3 * TIME_HEADS * HEAD_DIM)):
        width = TIME_HEADS * HEAD_DIM
        first = piece * 3 * width
        at = slice(piece * width, (piece + 1) * width)
        out_ref[:, at] = flat_rows(back_ref[:, :, first : first + width]).astype(BF16)
        first = first + width
        query_ref[:, at] = (flat_rows(back_ref[:, :, first : first + width]) + qs_ref[:, at]).astype(BF16)
        first = first + width
        key_ref[:, at] = (flat_rows(back_ref[:, :, first : first + width]) + ks_ref[:, at]).astype(BF16)


def exchange(chunks):
    return lax.all_to_all(chunks, "tm", split_axis=0, concat_axis=0, tiled=True)


def on_device(queries, key_states, value_states, out_grad):
    band_rows, breadth, channels = queries.shape[1:]
    tokens = band_rows * breadth
    rim = RADIUS * breadth
    parts = lax.axis_size("tm")
    bands = lax.axis_size("rows")
    spots = tokens // parts
    first_row = (lax.axis_index("rows") * band_rows).astype(jnp.int32).reshape(1)
    total_rows = bands * band_rows
    upward = [(i, i + 1) for i in range(bands - 1)]
    downward = [(i + 1, i) for i in range(bands - 1)]

    def chunks_of(tensor):
        return tensor.reshape(parts, spots, channels)

    moved = exchange(
        jnp.concatenate([chunks_of(queries), chunks_of(key_states), chunks_of(out_grad)], 2)
    )

    query, key, value = (
        tensor.reshape(tokens, channels) for tensor in (queries, key_states, value_states)
    )
    low = lax.ppermute(jnp.concatenate([key[tokens - rim :], value[tokens - rim :]], 0), "rows", upward)
    high = lax.ppermute(jnp.concatenate([key[:rim], value[:rim]], 0), "rows", downward)

    scalar = pl.BlockSpec(memory_space=pltpu.SMEM)

    def rows_block(rows, heads):
        return pl.BlockSpec((rows, heads * HEAD_DIM), lambda i: (0, i))

    def chunk_block(heads, offset, stride=1):
        return pl.BlockSpec((parts, spots, heads * HEAD_DIM), lambda i: (0, 0, i * stride + offset))

    def band_specs(heads):
        own = rows_block(tokens, heads)
        return [scalar, own, own, own, rows_block(2 * rim, heads), rows_block(2 * rim, heads)]

    sent = call(
        functools.partial(spatial_fwd_kernel, total_rows, breadth),
        HEADS // FWD_HEADS,
        band_specs(FWD_HEADS),
        chunk_block(FWD_HEADS, 0),
        jax.ShapeDtypeStruct((parts, spots, 2 * channels), BF16),
    )(first_row, query, key, value, low, high)

    count = HEADS // SCORE_HEADS
    sent, probs = call(
        temporal_scores_kernel,
        count,
        [chunk_block(SCORE_HEADS, place * count) for place in range(3)]
        + [pl.BlockSpec(memory_space=pl.ANY)],
        [
            chunk_block(SCORE_HEADS, count),
            pl.BlockSpec((SCORE_HEADS, tokens, tokens), lambda i: (i, 0, 0)),
        ],
        [
            jax.ShapeDtypeStruct(sent.shape, BF16),
            jax.ShapeDtypeStruct((HEADS, tokens, tokens), F32),
        ],
        input_output_aliases={3: 0},
    )(moved, moved, moved, sent)
    both = exchange(sent)

    count = HEADS // TIME_HEADS
    parts_out = call(
        temporal_grads_kernel,
        count,
        [chunk_block(TIME_HEADS, place * count) for place in range(3)]
        + [
            chunk_block(TIME_HEADS, 0),
            pl.BlockSpec((TIME_HEADS, tokens, tokens), lambda i: (i, 0, 0)),
        ],
        chunk_block(3 * TIME_HEADS, 0),
        jax.ShapeDtypeStruct((parts, spots, 3 * channels), BF16),
    )(moved, moved, moved, both, probs)
    parts_out, both = lax.optimization_barrier((parts_out, both))
    back = exchange(parts_out)

    count = HEADS // BWD_HEADS
    own = rows_block(tokens, BWD_HEADS)
    whole = jax.ShapeDtypeStruct((tokens, channels), F32)
    rims = jax.ShapeDtypeStruct((2 * rim, channels), BF16)
    qs, ks, vs, to_low, to_high = call(
        functools.partial(spatial_bwd_kernel, total_rows, breadth),
        count,
        band_specs(BWD_HEADS) + [chunk_block(BWD_HEADS, count)],
        [own, own, own, rows_block(2 * rim, BWD_HEADS), rows_block(2 * rim, BWD_HEADS)],
        [whole, whole, whole, rims, rims],
    )(first_row, query, key, value, low, high, both)
    from_high = lax.ppermute(to_low, "rows", downward)
    from_low = lax.ppermute(to_high, "rows", upward)
    final = jax.ShapeDtypeStruct((tokens, channels), BF16)
    own = rows_block(tokens, RIM_HEADS)
    ks, value_grad = call(
        rim_add_kernel,
        HEADS // RIM_HEADS,
        [own, own, rows_block(2 * rim, RIM_HEADS), rows_block(2 * rim, RIM_HEADS)],
        [own, own],
        [whole, final],
    )(ks, vs, from_low, from_high)

    own = rows_block(tokens, LAST_HEADS * 2)
    temporal_out, query_grad, key_grad = call(
        last_sum_kernel,
        HEADS // (LAST_HEADS * 2),
        [chunk_block(3 * LAST_HEADS * 2, 0), own, own],
        [own, own, own],
        [final, final, final],
    )(back, qs, ks)
    return tuple(
        tensor.reshape(queries.shape) for tensor in (temporal_out, query_grad, key_grad, value_grad)
    )


def solution(mesh):
    placed = P("tm", "rows", None, None)
    return jax.shard_map(
        on_device,
        mesh=mesh,
        in_specs=(placed,) * 4,
        out_specs=(placed,) * 4,
        check_vma=False,
    )
```

profile of v0, /device:TPU:6, one launch (start us, length us, event | category | flops | bytes accessed | tf_op | source)
XLA Modules:
  0.0 194.7 jit_solution(16627533711718905831)
XLA Ops:
  0.6 3.2 %pad_maximum_fusion = bf16[16,8,9216]{2,1,0:T(8,128)(2,1)} fusion(bf16[16,8,3072]{2,1,0:T(8,128)(2,1)} %bitcast.27, bf16[16,8,3072]{2,1,0:T(8,128)(2,1)} %bitcast.15, bf16[16,8,3072]{2,1,0:T(8,128)(2,1)} %bitcast.18), kind=kLoop, calls=%fused_computation | loop fusion | flops 7077888 | bytes 4718592 | tf_op jit(solution)/shard_map/concatenate | solution.py:215
  3.8 9.7 %all-to-all-start = ((bf16[16,8,9216]{2,1,0:T(8,128)(2,1)}), bf16[16,8,9216]{2,1,0:T(8,128)(2,1)S(1)}, u32[]{:S(2)}, u32[]{:S(2)}) async-start(bf16[16,8,9216]{2,1,0:T(8,128)(2,1)} %pad_maximum_fusion), calls=%async_computation | async-start | bytes 4718592 | tf_op jit(solution)/shard_map/all_to_all | solution.py:196
  13.6 1.1 copy-done.8
  15.6 1.9 collective-permute-start
  18.4 6.0 %collective-permute-start.1 = (bf16[96,3072]{1,0:T(8,128)(2,1)}, bf16[96,3072]{1,0:T(8,128)(2,1)}, u32[]{:S(2)}, u32[]{:S(2)}) collective-permute-start(bf16[96,3072]{1,0:T(8,128)(2,1)} %pad_maximum_fusion.2), channel_id=1, source_target_pairs={{1,0},{2,1},{3,2},{4,3},{5,4},{6,5},{7,6},{8,7},{9,8},{10,9},{11,1... | collective-permute-start | bytes 1769480 | tf_op jit(solution)/shard_map/ppermute | solution.py:222
  24.4 10.6 %collective-permute-done.low_ref = bf16[96,3072]{1,0:T(8,128)(2,1)} collective-permute-done((bf16[96,3072]{1,0:T(8,128)(2,1)}, bf16[96,3072]{1,0:T(8,128)(2,1)}, u32[]{:S(2)}, u32[]{:S(2)}) %collective-permute-start) | collective-permute-done | bytes 589856 | tf_op jit(solution)/shard_map/ppermute | solution.py:221
  35.0 1.1 copy-done.6
  36.2 1.1 copy-done.9
  37.3 9.2 %shard_map.75.sent_ref = bf16[16,8,6144]{2,1,0:T(8,128)(2,1)S(1)} custom-call(s32[1]{0:T(128)} %bitcast.3.first_ref, bf16[128,3072]{1,0:T(8,128)(2,1)S(1)} %bitcast.19, bf16[128,3072]{1,0:T(8,128)(2,1)S(1)} %bitcast.16, bf16[128,3072]{1,0:T(8,128)(2,1)S(1)} %bitcast.21, bf16[96,3072]{1,0:T(8,128)(2,1)} %collective-permute-done.low_ref, ...), custom_call_target="tpu_custom_call" | custom-call | tf_op jit(solution)/shard_map/pallas_call | solution.py:236
  46.6 1.1 copy-done.2
  47.7 20.8 %all-to-all-done.q_ref.k_ref.g_ref = bf16[16,8,9216]{2,1,0:T(8,128)(2,1)S(1)} async-done(((bf16[16,8,9216]{2,1,0:T(8,128)(2,1)}), bf16[16,8,9216]{2,1,0:T(8,128)(2,1)S(1)}, u32[]{:S(2)}, u32[]{:S(2)}) %all-to-all-start) | async-done | bytes 2359328 | tf_op jit(solution)/shard_map/all_to_all | solution.py:196
  68.5 1.4 copy-done.3
  69.9 6.3 %shard_map.76 = (bf16[16,8,6144]{2,1,0:T(8,128)(2,1)S(1)}, f32[24,128,128]{2,1,0:T(8,128)S(1)}) custom-call(bf16[16,8,9216]{2,1,0:T(8,128)(2,1)S(1)} %all-to-all-done.q_ref.k_ref.g_ref, bf16[16,8,9216]{2,1,0:T(8,128)(2,1)S(1)} %all-to-all-done.q_ref.k_ref.g_ref, ...), custom_call_target="tpu_custom_call", output_to_operand_aliasing={{0}: (3, {})} | custom-call | tf_op jit(solution)/shard_map/pallas_call | solution.py:245
  76.2 44.0 %all_to_all.15.s_ref.g_ref = bf16[16,8,6144]{2,1,0:T(8,128)(2,1)S(1)} all-to-all(bf16[16,8,6144]{2,1,0:T(8,128)(2,1)S(1)} %get-tuple-element.18), channel_id=1, replica_groups=mesh['tm'=16,'rows'=16] {'tm'}, dimensions={0} | all-to-all | bytes 3145728 | tf_op jit(solution)/shard_map/all_to_all | solution.py:196
  120.2 8.2 %shard_map.77 = bf16[16,8,9216]{2,1,0:T(8,128)(2,1)S(1)} custom-call(bf16[16,8,9216]{2,1,0:T(8,128)(2,1)} %copy-done, bf16[16,8,9216]{2,1,0:T(8,128)(2,1)} %copy-done, bf16[16,8,9216]{2,1,0:T(8,128)(2,1)} %copy-done, bf16[16,8,6144]{2,1,0:T(8,128)(2,1)S(1)} %all_to_all.15.s_ref.g_ref, f32[24,128,128]{2,1,0:T(8,128)S(1)} %get-tuple-element.19.probs_ref), custom_call_target="tpu_custom_call" | custom-call | tf_op jit(solution)/shard_map/pallas_call | solution.py:263
  128.4 1.4 copy-done.5
  129.8 4.8 %all-to-all-start.2 = ((bf16[16,8,9216]{2,1,0:T(8,128)(2,1)}), bf16[16,8,9216]{2,1,0:T(8,128)(2,1)S(1)}, u32[]{:S(2)}, u32[]{:S(2)}) async-start(bf16[16,8,9216]{2,1,0:T(8,128)(2,1)} %copy-done.5), calls=%async_computation.2 | async-start | bytes 4718592 | tf_op jit(solution)/shard_map/all_to_all | solution.py:196
  134.7 1.1 copy-done.7
  135.8 1.1 copy-done.10
  136.9 11.2 %shard_map.78 = (f32[128,3072]{1,0:T(8,128)}, f32[128,3072]{1,0:T(8,128)}, f32[128,3072]{1,0:T(8,128)}, bf16[96,3072]{1,0:T(8,128)(2,1)S(1)}, bf16[96,3072]{1,0:T(8,128)(2,1)S(1)}) custom-call(s32[1]{0:T(128)} %bitcast.3.first_ref, bf16[128,3072]{1,0:T(8,128)(2,1)S(1)} %bitcast.20, bf16[128,3072]{1,0:T(8,128)(2,1)S(1)} %bitcast.17, ...), custom_call_target="tpu_custom_call" | custom-call | tf_op jit(solution)/shard_map/pallas_call | solution.py:281
  148.1 1.9 collective-permute-start.2
  150.1 6.0 %collective-permute-start.3 = (bf16[96,3072]{1,0:T(8,128)(2,1)S(1)}, bf16[96,3072]{1,0:T(8,128)(2,1)S(1)}, u32[]{:S(2)}, u32[]{:S(2)}) collective-permute-start(bf16[96,3072]{1,0:T(8,128)(2,1)S(1)} %get-tuple-element.26), channel_id=1, source_target_pairs={{1,0},{2,1},{3,2},{4,3},{5,4},{6,5},{7,6},{8,7},{9,8},{10,9},{11,1... | collective-permute-start | bytes 1769480 | tf_op jit(solution)/shard_map/ppermute | solution.py:288
  156.1 8.8 %collective-permute-done.2.from_low_ref = bf16[96,3072]{1,0:T(8,128)(2,1)S(1)} collective-permute-done((bf16[96,3072]{1,0:T(8,128)(2,1)S(1)}, bf16[96,3072]{1,0:T(8,128)(2,1)S(1)}, u32[]{:S(2)}, u32[]{:S(2)}) %collective-permute-start.2) | collective-permute-done | bytes 589856 | tf_op jit(solution)/shard_map/ppermute | solution.py:289
  164.9 4.6 %collective-permute-done.3.from_high_ref = bf16[96,3072]{1,0:T(8,128)(2,1)S(1)} collective-permute-done((bf16[96,3072]{1,0:T(8,128)(2,1)S(1)}, bf16[96,3072]{1,0:T(8,128)(2,1)S(1)}, u32[]{:S(2)}, u32[]{:S(2)}) %collective-permute-start.3) | collective-permute-done | bytes 589856 | tf_op jit(solution)/shard_map/ppermute | solution.py:288
  169.5 1.4 copy-done.11
  170.9 1.4 copy-done.12
  172.3 1.8 shard_map.79
  174.2 1.1 copy-done.14
  175.3 14.7 %all-to-all-done.2.back_ref = bf16[16,8,9216]{2,1,0:T(8,128)(2,1)S(1)} async-done(((bf16[16,8,9216]{2,1,0:T(8,128)(2,1)}), bf16[16,8,9216]{2,1,0:T(8,128)(2,1)S(1)}, u32[]{:S(2)}, u32[]{:S(2)}) %all-to-all-start.2) | async-done | bytes 2359328 | tf_op jit(solution)/shard_map/all_to_all | solution.py:196
  190.0 1.4 copy-done.13
  191.4 1.4 copy-done.15
  192.8 1.9 shard_map.80
  (24 shorter events, 1.8 us)
Async XLA Ops:
  3.8 9.7 %copy-start.4 = (bf16[1,8,16,3072]{3,2,1,0:T(8,128)(2,1)S(1)}, bf16[1,8,16,3072]{3,2,1,0:T(8,128)(2,1)}, u32[]{:S(2)}) copy-start(bf16[1,8,16,3072]{3,2,1,0:T(8,128)(2,1)} %param.5) | copy-start | bytes 2359300
  3.8 64.7 %all-to-all-start = ((bf16[16,8,9216]{2,1,0:T(8,128)(2,1)}), bf16[16,8,9216]{2,1,0:T(8,128)(2,1)S(1)}, u32[]{:S(2)}, u32[]{:S(2)}) async-start(bf16[16,8,9216]{2,1,0:T(8,128)(2,1)} %pad_maximum_fusion), calls=%async_computation | async-start | bytes 4718592 | tf_op jit(solution)/shard_map/all_to_all | solution.py:196
  13.6 1.1 copy-start.8
  15.6 19.4 %collective-permute-start = (bf16[96,3072]{1,0:T(8,128)(2,1)}, bf16[96,3072]{1,0:T(8,128)(2,1)}, u32[]{:S(2)}, u32[]{:S(2)}) collective-permute-start(bf16[96,3072]{1,0:T(8,128)(2,1)} %pad_maximum_fusion.1), channel_id=1, source_target_pairs={{0,1},{1,2},{2,3},{3,4},{4,5},{5,6},{6,7},{7,8},{8,9},{9,10},{10,1... | collective-permute-start | bytes 1769480 | tf_op jit(solution)/shard_map/ppermute | solution.py:221
  18.4 16.7 %collective-permute-start.1 = (bf16[96,3072]{1,0:T(8,128)(2,1)}, bf16[96,3072]{1,0:T(8,128)(2,1)}, u32[]{:S(2)}, u32[]{:S(2)}) collective-permute-start(bf16[96,3072]{1,0:T(8,128)(2,1)} %pad_maximum_fusion.2), channel_id=1, source_target_pairs={{1,0},{2,1},{3,2},{4,3},{5,4},{6,5},{7,6},{8,7},{9,8},{10,9},{11,1... | collective-permute-start | bytes 1769480 | tf_op jit(solution)/shard_map/ppermute | solution.py:222
  35.0 1.1 copy-start.6
  36.2 1.1 copy-start.9
  46.6 1.2 copy-start.2
  68.5 1.4 copy-start.3
  69.9 6.3 %copy-start = (bf16[16,8,9216]{2,1,0:T(8,128)(2,1)}, bf16[16,8,9216]{2,1,0:T(8,128)(2,1)S(1)}, u32[]{:S(2)}) copy-start(bf16[16,8,9216]{2,1,0:T(8,128)(2,1)S(1)} %all-to-all-done.q_ref.k_ref.g_ref) | copy-start | bytes 7077892
  120.2 8.2 %copy-start.1 = (bf16[16,8,6144]{2,1,0:T(8,128)(2,1)}, bf16[16,8,6144]{2,1,0:T(8,128)(2,1)S(1)}, u32[]{:S(2)}) copy-start(bf16[16,8,6144]{2,1,0:T(8,128)(2,1)S(1)} %all_to_all.15.s_ref.g_ref) | copy-start | bytes 4718596
  128.4 1.4 copy-start.5
  129.8 60.2 %all-to-all-start.2 = ((bf16[16,8,9216]{2,1,0:T(8,128)(2,1)}), bf16[16,8,9216]{2,1,0:T(8,128)(2,1)S(1)}, u32[]{:S(2)}, u32[]{:S(2)}) async-start(bf16[16,8,9216]{2,1,0:T(8,128)(2,1)} %copy-done.5), calls=%async_computation.2 | async-start | bytes 4718592 | tf_op jit(solution)/shard_map/all_to_all | solution.py:196
  134.7 1.1 copy-start.7
  135.8 1.1 copy-start.10
  148.1 16.8 %collective-permute-start.2 = (bf16[96,3072]{1,0:T(8,128)(2,1)S(1)}, bf16[96,3072]{1,0:T(8,128)(2,1)S(1)}, u32[]{:S(2)}, u32[]{:S(2)}) collective-permute-start(bf16[96,3072]{1,0:T(8,128)(2,1)S(1)} %get-tuple-element.25), channel_id=1, source_target_pairs={{0,1},{1,2},{2,3},{3,4},{4,5},{5,6},{6,7},{7,8},{8,9},{9,10},{10,1... | collective-permute-start | bytes 1769480 | tf_op jit(solution)/shard_map/ppermute | solution.py:289
  150.1 19.4 %collective-permute-start.3 = (bf16[96,3072]{1,0:T(8,128)(2,1)S(1)}, bf16[96,3072]{1,0:T(8,128)(2,1)S(1)}, u32[]{:S(2)}, u32[]{:S(2)}) collective-permute-start(bf16[96,3072]{1,0:T(8,128)(2,1)S(1)} %get-tuple-element.26), channel_id=1, source_target_pairs={{1,0},{2,1},{3,2},{4,3},{5,4},{6,5},{7,6},{8,7},{9,8},{10,9},{11,1... | collective-permute-start | bytes 1769480 | tf_op jit(solution)/shard_map/ppermute | solution.py:288
  169.5 1.4 copy-start.11
  170.9 1.4 copy-start.12
  174.2 1.2 copy-start.14
  190.0 1.4 copy-start.13
  191.4 1.4 copy-start.15
where the time goes:
time: 196 us; the launch traced here: 195 us
  waiting for transfers between devices  59.5 us (30%)
  blocking collectives  44 us (22%)
  Pallas kernels  38.7 us (20%)
  starting transfers between devices  30.4 us (16%)
  local copies, waits for them, and re-layouts  16.5 us (8%)
  other arithmetic  4.92 us (3%)
    all_to_all x1, blocking collectives, exchange(): return lax.all_to_all(chunks, 'tm', split_axis=0, concat_axis=0, tiled=True)  44 us
    all_to_all x2, waiting for transfers between devices, exchange(): return lax.all_to_all(chunks, 'tm', split_axis=0, concat_axis=0, tiled=True)  35.5 us
    unnamed x32, local copies, waits for them, and re-layouts  16.4 us
    all_to_all x2, starting transfers between devices, exchange(): return lax.all_to_all(chunks, 'tm', split_axis=0, concat_axis=0, tiled=True)  14.5 us
    pallas_call x1, Pallas kernels, on_device(): call(functools.partial(spatial_bwd_kernel, total_rows, breadth), count, b...  11.2 us
    ppermute x1, waiting for transfers between devices, on_device(): lax.ppermute(jnp.concatenate([key[tokens - rim:], value[tokens - rim:]],...  10.6 us
    pallas_call x1, Pallas kernels, on_device(): call(functools.partial(spatial_fwd_kernel, total_rows, breadth), HEADS //...  9.23 us
    ppermute x1, waiting for transfers between devices, on_device(): from_low = lax.ppermute(to_high, 'rows', upward)  8.79 us
  transfers between devices with their start and end apart: 6, of which 5 were waited for; matrix products, arithmetic and copies ran while one was open for 1% of the time, Pallas kernels for 11%

commit v1 on v0

v1 whole, which is shorter than its diff:
```python
import functools

import jax
import jax.numpy as jnp
from jax import lax
from jax.experimental import pallas as pl
from jax.experimental.pallas import tpu as pltpu
from jax.sharding import PartitionSpec as P

HEADS = 24
HEAD_DIM = 128
RADIUS = 3
SCALING = HEAD_DIM ** (-0.5)
NEG_FILL = -1e30
BF16 = jnp.bfloat16
F32 = jnp.float32

FWD_HEADS = 4
SCORE_HEADS = 8
TIME_HEADS = 8
BWD_HEADS = 4
RIM_HEADS = 8
PIECES = 4

NT = (((1,), (1,)), ((), ()))
NN = (((1,), (0,)), ((), ()))
TN = (((0,), (0,)), ((), ()))


def dot(left, right, dims):
    return lax.dot_general(left, right, dims, preferred_element_type=F32)


def lanes(head):
    return slice(head * HEAD_DIM, (head + 1) * HEAD_DIM)


def flat_rows(chunks):
    wide = chunks.astype(F32)
    return wide.reshape(wide.shape[0] * wide.shape[1], wide.shape[2])


def head_rows(ref, head):
    return flat_rows(ref[:, :, lanes(head)]).astype(BF16)


def chunked(matrix, chunks):
    return matrix.reshape(chunks, matrix.shape[0] // chunks, matrix.shape[1])


def softmax_columns(scores):
    peak = jnp.max(scores, 0, keepdims=True)
    grown = jnp.exp((scores - peak) * SCALING)
    return grown * (1.0 / jnp.sum(grown, 0, keepdims=True))


params = pltpu.CompilerParams(vmem_limit_bytes=16 * 1024 * 1024)


def call(kernel, grid, in_specs, out_specs, out_shape, **more):
    return pl.pallas_call(
        kernel,
        grid=(grid,),
        in_specs=in_specs,
        out_specs=out_specs,
        out_shape=out_shape,
        compiler_params=params,
        **more,
    )


def window_mask(first_row, total_rows, breadth, keys, queries, reach=RADIUS):
    key = lax.broadcasted_iota(jnp.int32, (keys, queries), 0)
    query = lax.broadcasted_iota(jnp.int32, (keys, queries), 1)
    row_step = key // breadth - reach - query // breadth
    col_step = key % breadth - query % breadth
    key_row = first_row - reach + key // breadth
    return (
        (jnp.abs(row_step) <= RADIUS)
        & (jnp.abs(col_step) <= RADIUS)
        & (key_row >= 0)
        & (key_row < total_rows)
    )


def window_of(own_ref, low_ref, high_ref, half, head):
    at = lanes(head)
    return jnp.concatenate([low_ref[half, :, at], own_ref[:, at], high_ref[half, :, at]], 0)


def spatial_fwd_kernel(total_rows, breadth, first_ref, q_ref, k_ref, v_ref, low_ref, high_ref, s_ref):
    queries = q_ref.shape[0]
    keys = queries + 2 * low_ref.shape[1]
    allowed = window_mask(first_ref[0], total_rows, breadth, keys, queries)
    heads = range(q_ref.shape[1] // HEAD_DIM)
    scores = [
        dot(window_of(k_ref, low_ref, high_ref, 0, head), q_ref[:, lanes(head)], NT) for head in heads
    ]
    weights = [softmax_columns(jnp.where(allowed, part, NEG_FILL)).astype(BF16) for part in scores]
    outs = [dot(weights[head], window_of(v_ref, low_ref, high_ref, 1, head), TN) for head in heads]
    for head in heads:
        s_ref[:, :, lanes(head)] = chunked(outs[head], s_ref.shape[0]).astype(BF16)


def spatial_bwd_kernel(
    total_rows, breadth, first_ref, q_ref, k_ref, v_ref, low_ref, high_ref, g_ref,
    qs_ref, ks_ref, vs_ref, to_low_ref, to_high_ref,
):
    queries = q_ref.shape[0]
    rim = low_ref.shape[1]
    keys = queries + 2 * rim
    allowed = window_mask(first_ref[0], total_rows, breadth, keys, queries)
    heads = range(q_ref.shape[1] // HEAD_DIM)
    scores = [
        dot(window_of(k_ref, low_ref, high_ref, 0, head), q_ref[:, lanes(head)], NT) for head in heads
    ]
    grads = [head_rows(g_ref, head) for head in heads]
    prob_grads = [
        dot(window_of(v_ref, low_ref, high_ref, 1, head), grads[head], NT) for head in heads
    ]
    weights, score_grads = [], []
    for head in heads:
        probs = softmax_columns(jnp.where(allowed, scores[head], NEG_FILL))
        weights.append(probs.astype(BF16))
        grad_dot = jnp.sum(weights[head].astype(F32) * prob_grads[head], 0, keepdims=True)
        score_grads.append((probs * (prob_grads[head] - grad_dot)).astype(BF16))
    values = [dot(weights[head], grads[head], NN) for head in heads]
    keys = [dot(score_grads[head], q_ref[:, lanes(head)], NN) * SCALING for head in heads]
    for wide, own_ref, half in (
        (keys, ks_ref, 0),
        (values, vs_ref, 1),
    ):
        for head in heads:
            at = lanes(head)
            own_ref[:, at] = wide[head][rim : rim + queries]
            to_low_ref[half, :, at] = wide[head][:rim].astype(BF16)
            to_high_ref[half, :, at] = wide[head][rim + queries :].astype(BF16)
    for head in heads:
        key = window_of(k_ref, low_ref, high_ref, 0, head)
        qs_ref[:, lanes(head)] = dot(score_grads[head], key, TN) * SCALING


def same_position(rows, spots):
    left = lax.broadcasted_iota(jnp.int32, (rows, rows), 0)
    right = lax.broadcasted_iota(jnp.int32, (rows, rows), 1)
    return left % spots == right % spots


def temporal_scores_kernel(q_ref, k_ref, g_ref, sent_ref, grad_ref, probs_ref):
    del sent_ref
    frames, spots = q_ref.shape[0], q_ref.shape[1]
    same = same_position(frames * spots, spots)
    heads = range(q_ref.shape[2] // HEAD_DIM)
    scores = [dot(head_rows(k_ref, head), head_rows(q_ref, head), NT) for head in heads]
    probs = [softmax_columns(jnp.where(same, part, NEG_FILL)) for part in scores]
    grads = [dot(probs[head].astype(BF16), head_rows(g_ref, head), NN) for head in heads]
    for head in heads:
        probs_ref[head] = probs[head]
    for head in heads:
        grad_ref[:, :, lanes(head)] = chunked(grads[head], frames).astype(BF16)


def temporal_grads_kernel(q_ref, k_ref, g_ref, s_ref, probs_ref, out_ref):
    frames = q_ref.shape[0]
    width = q_ref.shape[2]
    heads = range(width // HEAD_DIM)
    spatial = [head_rows(s_ref, head) for head in heads]
    prob_grads = [dot(spatial[head], head_rows(g_ref, head), NT) for head in heads]
    outs = [dot(probs_ref[head].astype(BF16), spatial[head], TN) for head in heads]
    score_grads = []
    for head in heads:
        probs = probs_ref[head]
        weights = probs.astype(BF16).astype(F32)
        grad_dot = jnp.sum(weights * prob_grads[head], 0, keepdims=True)
        score_grads.append((probs * (prob_grads[head] - grad_dot)).astype(BF16))
    query_parts = [dot(score_grads[head], head_rows(k_ref, head), TN) * SCALING for head in heads]
    key_parts = [dot(score_grads[head], head_rows(q_ref, head), NN) * SCALING for head in heads]
    for place, parts in enumerate((outs, query_parts, key_parts)):
        for head in heads:
            first = place * width + head * HEAD_DIM
            out_ref[:, :, first : first + HEAD_DIM] = chunked(parts[head], frames).astype(BF16)


def rims_kernel(k_first_ref, v_first_ref, k_last_ref, v_last_ref, to_low_ref, to_high_ref):
    to_low_ref[0] = k_first_ref[...]
    to_low_ref[1] = v_first_ref[...]
    to_high_ref[0] = k_last_ref[...]
    to_high_ref[1] = v_last_ref[...]


def started(source, target, sem):
    copy = pltpu.make_async_copy(source, target, sem)
    copy.start()
    return copy


def join_kernel(*refs):
    sources, (joined_ref, held, load_sems, store_sems) = refs[:-4], refs[-4:]
    pieces = load_sems.shape[0]
    chunks, width = joined_ref.shape[0] // pieces, sources[0].shape[2]
    loads = []
    for piece in range(pieces):
        rows = slice(piece * chunks, (piece + 1) * chunks)
        loads.append(
            [
                started(
                    source.at[rows],
                    held.at[rows, :, place * width : (place + 1) * width],
                    load_sems.at[piece, place],
                )
                for place, source in enumerate(sources)
            ]
        )
    stores = []
    for piece in range(pieces):
        rows = slice(piece * chunks, (piece + 1) * chunks)
        for load in loads[piece]:
            load.wait()
        stores.append(started(held.at[rows], joined_ref.at[rows], store_sems.at[piece]))
    for store in stores:
        store.wait()


def rim_add_kernel(ks_ref, vs_ref, from_low_ref, from_high_ref, key_ref, value_ref):
    rim = from_low_ref.shape[1]
    rows = ks_ref.shape[0]
    for half, (sum_ref, out_ref) in enumerate(((ks_ref, key_ref), (vs_ref, value_ref))):
        out_ref[:rim] = (sum_ref[:rim] + from_low_ref[half].astype(F32)).astype(out_ref.dtype)
        out_ref[rim : rows - rim] = sum_ref[rim : rows - rim].astype(out_ref.dtype)
        out_ref[rows - rim :] = (sum_ref[rows - rim :] + from_high_ref[half].astype(F32)).astype(
            out_ref.dtype
        )


def last_sum_kernel(back_ref, qs_ref, ks_ref, *refs):
    outs, (back, qs, ks), results, (load_sems, store_sems) = refs[:3], refs[3:6], refs[6:9], refs[9:]
    pieces = load_sems.shape[0]
    chunks, rows = back.shape[0] // pieces, qs.shape[0] // pieces
    width = TIME_HEADS * HEAD_DIM
    loads, stores = [], []
    for piece in range(pieces):
        some = slice(piece * chunks, (piece + 1) * chunks)
        at = slice(piece * rows, (piece + 1) * rows)
        pairs = ((back_ref.at[some], back.at[some]), (qs_ref.at[at], qs.at[at]), (ks_ref.at[at], ks.at[at]))
        loads.append(
            [started(*pair, load_sems.at[piece, place]) for place, pair in enumerate(pairs)]
        )
    for piece in range(pieces):
        for load in loads[piece]:
            load.wait()
        some = slice(piece * chunks, (piece + 1) * chunks)
        at = slice(piece * rows, (piece + 1) * rows)
        for group in range(HEADS // TIME_HEADS):
            to = slice(group * width, (group + 1) * width)
            parts = [
                flat_rows(back[some, :, (group * 3 + place) * width : (group * 3 + place + 1) * width])
                for place in range(3)
            ]
            results[0][at, to] = parts[0].astype(BF16)
            results[1][at, to] = (parts[1] + qs[at, to]).astype(BF16)
            results[2][at, to] = (parts[2] + ks[at, to]).astype(BF16)
        for place in range(3):
            stores.append(
                started(results[place].at[at], outs[place].at[at], store_sems.at[piece, place])
            )
    for store in stores:
        store.wait()


def in_hbm(tensor):
    return pltpu.with_memory_space_constraint(tensor, pltpu.HBM)


def exchange(chunks):
    return lax.all_to_all(chunks, "tm", split_axis=0, concat_axis=0, tiled=True)


def on_device(queries, key_states, value_states, out_grad):
    band_rows, breadth, channels = queries.shape[1:]
    tokens = band_rows * breadth
    rim = RADIUS * breadth
    parts = lax.axis_size("tm")
    bands = lax.axis_size("rows")
    spots = tokens // parts
    band = lax.axis_index("rows").astype(jnp.int32)
    first_row = (band * band_rows).reshape(1)
    total_rows = bands * band_rows
    upward = [(i, i + 1) for i in range(bands - 1)]
    downward = [(i + 1, i) for i in range(bands - 1)]

    scalar = pl.BlockSpec(memory_space=pltpu.SMEM)
    anywhere = pl.BlockSpec(memory_space=pl.ANY)

    def rows_block(rows, heads):
        return pl.BlockSpec((rows, heads * HEAD_DIM), lambda i: (0, i))

    def rims_block(heads):
        return pl.BlockSpec((2, rim, heads * HEAD_DIM), lambda i: (0, 0, i))

    def chunk_block(heads, offset, stride=1):
        return pl.BlockSpec((parts, spots, heads * HEAD_DIM), lambda i: (0, 0, i * stride + offset))

    query, key, value = (
        tensor.reshape(tokens, channels) for tensor in (queries, key_states, value_states)
    )
    rims = jax.ShapeDtypeStruct((2, rim, channels), BF16)
    first_rows = pl.BlockSpec((breadth, channels), lambda i: (i, 0))
    last_rows = pl.BlockSpec((breadth, channels), lambda i: (i + band_rows - RADIUS, 0))
    rim_rows = pl.BlockSpec((2, breadth, channels), lambda i: (0, i, 0))
    to_low, to_high = call(
        rims_kernel,
        RADIUS,
        [first_rows, first_rows, last_rows, last_rows],
        [rim_rows, rim_rows],
        [pltpu.HBM(rims.shape, BF16)] * 2,
    )(*map(in_hbm, (key, value, key, value)))
    low = lax.ppermute(to_high, "rows", upward)
    high = lax.ppermute(to_low, "rows", downward)

    joined_shape = (parts, spots, 3 * channels)
    joined = pl.pallas_call(
        join_kernel,
        in_specs=[anywhere] * 3,
        out_specs=anywhere,
        out_shape=pltpu.HBM(joined_shape, BF16),
        scratch_shapes=[
            pltpu.VMEM(joined_shape, BF16),
            pltpu.SemaphoreType.DMA((PIECES, 3)),
            pltpu.SemaphoreType.DMA((PIECES,)),
        ],
        compiler_params=params,
    )(*(in_hbm(tensor.reshape(parts, spots, channels)) for tensor in (queries, key_states, out_grad)))
    moved = exchange(joined)

    own = rows_block(tokens, FWD_HEADS)
    sent = call(
        functools.partial(spatial_fwd_kernel, total_rows, breadth),
        HEADS // FWD_HEADS,
        [scalar, own, own, own, rims_block(FWD_HEADS), rims_block(FWD_HEADS)],
        chunk_block(FWD_HEADS, 0),
        pltpu.HBM((parts, spots, 2 * channels), BF16),
    )(first_row, query, key, value, low, high)

    count = HEADS // SCORE_HEADS
    sent, probs = call(
        temporal_scores_kernel,
        count,
        [chunk_block(SCORE_HEADS, place * count) for place in range(3)]
        + [anywhere],
        [
            chunk_block(SCORE_HEADS, count),
            pl.BlockSpec((SCORE_HEADS, tokens, tokens), lambda i: (i, 0, 0)),
        ],
        [
            pltpu.HBM(sent.shape, BF16),
            jax.ShapeDtypeStruct((HEADS, tokens, tokens), F32),
        ],
        input_output_aliases={3: 0},
    )(moved, moved, moved, sent)
    both = in_hbm(exchange(sent))

    count = HEADS // TIME_HEADS
    parts_out = call(
        temporal_grads_kernel,
        count,
        [chunk_block(TIME_HEADS, place * count) for place in range(3)]
        + [
            chunk_block(TIME_HEADS, 0),
            pl.BlockSpec((TIME_HEADS, tokens, tokens), lambda i: (i, 0, 0)),
        ],
        chunk_block(3 * TIME_HEADS, 0),
        pltpu.HBM((parts, spots, 3 * channels), BF16),
    )(moved, moved, moved, both, probs)
    parts_out, both = lax.optimization_barrier((parts_out, both))
    back = exchange(parts_out)

    count = HEADS // BWD_HEADS
    own = rows_block(tokens, BWD_HEADS)
    whole = jax.ShapeDtypeStruct((tokens, channels), F32)
    qs, ks, vs, to_low, to_high = call(
        functools.partial(spatial_bwd_kernel, total_rows, breadth),
        count,
        [scalar, own, own, own, rims_block(BWD_HEADS), rims_block(BWD_HEADS), chunk_block(BWD_HEADS, count)],
        [own, own, own, rims_block(BWD_HEADS), rims_block(BWD_HEADS)],
        [pltpu.HBM((tokens, channels), F32), whole, whole, rims, rims],
    )(first_row, query, key, value, low, high, in_hbm(both))
    from_high = lax.ppermute(to_low, "rows", downward)
    from_low = lax.ppermute(to_high, "rows", upward)
    final = jax.ShapeDtypeStruct((tokens, channels), BF16)
    own = rows_block(tokens, RIM_HEADS)
    ks, value_grad = call(
        rim_add_kernel,
        HEADS // RIM_HEADS,
        [own, own, rims_block(RIM_HEADS), rims_block(RIM_HEADS)],
        [own, own],
        [pltpu.HBM((tokens, channels), F32), final],
    )(ks, vs, from_low, from_high)

    temporal_out, query_grad, key_grad = pl.pallas_call(
        last_sum_kernel,
        in_specs=[anywhere] * 3,
        out_specs=[anywhere] * 3,
        out_shape=[pltpu.HBM((tokens, channels), BF16)] * 3,
        scratch_shapes=[pltpu.VMEM(joined_shape, BF16)]
        + [pltpu.VMEM((tokens, channels), F32)] * 2
        + [pltpu.VMEM((tokens, channels), BF16)] * 3
        + [pltpu.SemaphoreType.DMA((PIECES, 3))] * 2,
        compiler_params=params,
    )(back, in_hbm(qs), in_hbm(ks))
    return tuple(
        tensor.reshape(queries.shape) for tensor in (temporal_out, query_grad, key_grad, value_grad)
    )


def solution(mesh):
    placed = P("tm", "rows", None, None)
    return jax.shard_map(
        on_device,
        mesh=mesh,
        in_specs=(placed,) * 4,
        out_specs=(placed,) * 4,
        check_vma=False,
    )
```

time: 196 us -> 185 us (0.944)
  local copies, waits for them, and re-layouts: 16.5 us -> 2.28 us
  waiting for transfers between devices: 59.5 us -> 73.4 us
  Pallas kernels: 38.7 us -> 32.5 us
  other arithmetic: 4.92 us -> 0 us
    all_to_all x2, waiting for transfers between devices: 35.5 us -> 54.3 us  [exchange(): return lax.all_to_all(chunks, 'tm', split_axis=0, concat_axis=0, tiled=True)]
    unnamed x32 -> x10, local copies, waits for them, and re-layouts: 16.4 us -> 2.28 us
    concatenate x3 -> x0, other arithmetic: 4.92 us -> none  [the longest x1 3.2 us: on_device(): jnp.concatenate([chunks_of(queries), chunks_of(key_states), chunks_of(out...]
    pallas_call x3 -> x5, Pallas kernels: 15 us -> 19.2 us  [the longest x1 7.06 us: on_device(): call(functools.partial(spatial_bwd_kernel, total_rows, breadth), count, [...]
    pallas_call x1, Pallas kernels: 8.19 us -> 4.45 us  [on_device(): call(temporal_grads_kernel, count, [chunk_block(TIME_HEADS, place * count...]
    pallas_call x1, Pallas kernels: 6.26 us -> 2.7 us  [on_device(): call(temporal_scores_kernel, count, [chunk_block(SCORE_HEADS, place * cou...]
    pallas_call x1, Pallas kernels: 9.23 us -> 6.17 us  [on_device(): call(functools.partial(spatial_fwd_kernel, total_rows, breadth), HEADS //...]
    ppermute x1, waiting for transfers between devices: 4.59 us -> 1.55 us  [on_device(): from_high = lax.ppermute(to_low, 'rows', downward)]
  transfers between devices with their start and end apart: 6 -> 6, of which waited for: 5 -> 5; matrix products, arithmetic and copies ran while one was open for 1% -> 0% of each run, Pallas kernels for 11% -> 10%
where the time goes in v1:
time: 185 us; the launch traced here: 184 us
  waiting for transfers between devices  73.4 us (40%)
  blocking collectives  44.3 us (24%)
  Pallas kernels  32.5 us (18%)
  starting transfers between devices  30.5 us (16%)
  local copies, waits for them, and re-layouts  2.28 us (1%)
    all_to_all x2, waiting for transfers between devices, exchange(): return lax.all_to_all(chunks, 'tm', split_axis=0, concat_axis=0, tiled=True)  54.3 us
    all_to_all x1, blocking collectives, exchange(): return lax.all_to_all(chunks, 'tm', split_axis=0, concat_axis=0, tiled=True)  44.3 us
    all_to_all x2, starting transfers between devices, exchange(): return lax.all_to_all(chunks, 'tm', split_axis=0, concat_axis=0, tiled=True)  14.6 us
    ppermute x1, waiting for transfers between devices, on_device(): low = lax.ppermute(to_high, 'rows', upward)  10.2 us
    ppermute x1, waiting for transfers between devices, on_device(): from_low = lax.ppermute(to_high, 'rows', upward)  7.37 us
    pallas_call x1, Pallas kernels, on_device(): call(functools.partial(spatial_bwd_kernel, total_rows, breadth), count, [...  7.06 us
    pallas_call x1, Pallas kernels, on_device(): call(functools.partial(spatial_fwd_kernel, total_rows, breadth), HEADS //...  6.17 us
    ppermute x1, starting transfers between devices, on_device(): high = lax.ppermute(to_low, 'rows', downward)  6.05 us
  transfers between devices with their start and end apart: 6, of which 5 were waited for; matrix products, arithmetic and copies ran while one was open for 0% of the time, Pallas kernels for 10%

profile of v1, /device:TPU:6, one launch (start us, length us, event | category | flops | bytes accessed | tf_op | source)
XLA Modules:
  0.0 183.7 jit_solution(18019370343954075504)
XLA Ops:
  0.6 2.7 %shard_map.75 = bf16[16,8,9216]{2,1,0:T(8,128)(2,1)} custom-call(bf16[16,8,3072]{2,1,0:T(8,128)(2,1)} %bitcast.20, bf16[16,8,3072]{2,1,0:T(8,128)(2,1)} %bitcast.11, bf16[16,8,3072]{2,1,0:T(8,128)(2,1)} %bitcast.23), custom_call_target="tpu_custom_call" | custom-call | tf_op jit(solution)/shard_map/pallas_call | solution.py:321
  3.4 9.6 %all-to-all-start = ((bf16[16,8,9216]{2,1,0:T(8,128)(2,1)}), bf16[16,8,9216]{2,1,0:T(8,128)(2,1)S(1)}, u32[]{:S(2)}, u32[]{:S(2)}) async-start(bf16[16,8,9216]{2,1,0:T(8,128)(2,1)} %shard_map.75), calls=%async_computation | async-start | bytes 4718592 | tf_op jit(solution)/shard_map/all_to_all | solution.py:275
  13.0 0.0 copy-start
  13.0 3.3 %shard_map.76 = (bf16[2,48,3072]{2,1,0:T(8,128)(2,1)}, bf16[2,48,3072]{2,1,0:T(8,128)(2,1)}) custom-call(bf16[128,3072]{1,0:T(8,128)(2,1)} %bitcast.12, bf16[128,3072]{1,0:T(8,128)(2,1)} %bitcast.16, bf16[128,3072]{1,0:T(8,128)(2,1)} %bitcast.13, bf16[128,3072]{1,0:T(8,128)(2,1)} %bitcast.17), custom_call_target="tpu_custom_call" | custom-call | tf_op jit(solution)/shard_map/pallas_call | solution.py:310
  16.3 1.9 %collective-permute-start = (bf16[2,48,3072]{2,1,0:T(8,128)(2,1)}, bf16[2,48,3072]{2,1,0:T(8,128)(2,1)}, u32[]{:S(2)}, u32[]{:S(2)}) collective-permute-start(bf16[2,48,3072]{2,1,0:T(8,128)(2,1)} %get-tuple-element.20), channel_id=1, source_target_pairs={{0,1},{1,2},{2,3},{3,4},{4,5},{5,6},{6,7},{7,8},{8,9},{9,10},{10,1... | collective-permute-start | bytes 1769480 | tf_op jit(solution)/shard_map/ppermute | solution.py:317
  18.2 6.0 %collective-permute-start.1 = (bf16[2,48,3072]{2,1,0:T(8,128)(2,1)}, bf16[2,48,3072]{2,1,0:T(8,128)(2,1)}, u32[]{:S(2)}, u32[]{:S(2)}) collective-permute-start(bf16[2,48,3072]{2,1,0:T(8,128)(2,1)} %get-tuple-element.21), channel_id=1, source_target_pairs={{1,0},{2,1},{3,2},{4,3},{5,4},{6,5},{7,6},{8,7},{9,8},{10,9},{11,1... | collective-permute-start | bytes 1769480 | tf_op jit(solution)/shard_map/ppermute | solution.py:318
  24.2 10.2 %collective-permute-done.low_ref = bf16[2,48,3072]{2,1,0:T(8,128)(2,1)} collective-permute-done((bf16[2,48,3072]{2,1,0:T(8,128)(2,1)}, bf16[2,48,3072]{2,1,0:T(8,128)(2,1)}, u32[]{:S(2)}, u32[]{:S(2)}) %collective-permute-start) | collective-permute-done | bytes 589856 | tf_op jit(solution)/shard_map/ppermute | solution.py:317
  34.5 0.0 collective-permute-done.1.high_ref
  34.5 0.0 copy-done
  34.5 0.0 copy-start.1
  34.5 1.1 copy-done.1
  35.6 0.0 copy-start.3
  35.6 1.1 copy-done.3
  36.7 6.2 %shard_map.77.sent_ref = bf16[16,8,6144]{2,1,0:T(8,128)(2,1)} custom-call(s32[1]{0:T(128)} %bitcast.3.first_ref, bf16[128,3072]{1,0:T(8,128)(2,1)S(1)} %bitcast.21, bf16[128,3072]{1,0:T(8,128)(2,1)S(1)} %bitcast.14, bf16[128,3072]{1,0:T(8,128)(2,1)S(1)} %bitcast.18, bf16[2,48,3072]{2,1,0:T(8,128)(2,1)} %collective-permute-done.low_ref, ...), custom_call_target="tpu_custom_call" | custom-call | tf_op jit(solution)/shard_map/pallas_call | solution.py:336
  42.9 25.0 %all-to-all-done.q_ref.k_ref.g_ref = bf16[16,8,9216]{2,1,0:T(8,128)(2,1)S(1)} async-done(((bf16[16,8,9216]{2,1,0:T(8,128)(2,1)}), bf16[16,8,9216]{2,1,0:T(8,128)(2,1)S(1)}, u32[]{:S(2)}, u32[]{:S(2)}) %all-to-all-start) | async-done | bytes 2359328 | tf_op jit(solution)/shard_map/all_to_all | solution.py:275
  67.9 2.7 %shard_map.78 = (bf16[16,8,6144]{2,1,0:T(8,128)(2,1)}, f32[24,128,128]{2,1,0:T(8,128)S(1)}) custom-call(bf16[16,8,9216]{2,1,0:T(8,128)(2,1)S(1)} %all-to-all-done.q_ref.k_ref.g_ref, bf16[16,8,9216]{2,1,0:T(8,128)(2,1)S(1)} %all-to-all-done.q_ref.k_ref.g_ref, ...), custom_call_target="tpu_custom_call", output_to_operand_aliasing={{0}: (3, {})} | custom-call | tf_op jit(solution)/shard_map/pallas_call | solution.py:345
  70.6 44.3 %all_to_all.15.s_ref.g_ref = bf16[16,8,6144]{2,1,0:T(8,128)(2,1)} all-to-all(bf16[16,8,6144]{2,1,0:T(8,128)(2,1)} %get-tuple-element.22), channel_id=1, replica_groups=mesh['tm'=16,'rows'=16] {'tm'}, dimensions={0} | all-to-all | bytes 3145728 | tf_op jit(solution)/shard_map/all_to_all | solution.py:275
  114.9 4.4 %shard_map.79 = bf16[16,8,9216]{2,1,0:T(8,128)(2,1)} custom-call(bf16[16,8,9216]{2,1,0:T(8,128)(2,1)S(1)} %all-to-all-done.q_ref.k_ref.g_ref, bf16[16,8,9216]{2,1,0:T(8,128)(2,1)S(1)} %all-to-all-done.q_ref.k_ref.g_ref, bf16[16,8,9216]{2,1,0:T(8,128)(2,1)S(1)} %all-to-all-done.q_ref.k_ref.g_ref, bf16[16,8,6144]{2,1,0:T(8,128)(2,1)} %all_to_all.15.s_ref.g_ref, ...), custom_call_target="tpu_custom_call" | custom-call | tf_op jit(solution)/shard_map/pallas_call | solution.py:363
  119.4 0.0 copy-start.2
  119.4 0.0 copy-start.4
  119.4 5.0 %all-to-all-start.2 = ((bf16[16,8,9216]{2,1,0:T(8,128)(2,1)}), bf16[16,8,9216]{2,1,0:T(8,128)(2,1)}, u32[]{:S(2)}, u32[]{:S(2)}) async-start(bf16[16,8,9216]{2,1,0:T(8,128)(2,1)} %shard_map.79), calls=%async_computation.2 | async-start | bytes 4718592 | tf_op jit(solution)/shard_map/all_to_all | solution.py:275
  124.4 0.0 copy-done.2
  124.4 0.0 copy-done.4
  124.4 7.1 %shard_map.80 = (f32[128,3072]{1,0:T(8,128)}, f32[128,3072]{1,0:T(8,128)S(1)}, f32[128,3072]{1,0:T(8,128)S(1)}, bf16[2,48,3072]{2,1,0:T(8,128)(2,1)S(1)}, bf16[2,48,3072]{2,1,0:T(8,128)(2,1)S(1)}) custom-call(s32[1]{0:T(128)} %bitcast.3.first_ref, bf16[128,3072]{1,0:T(8,128)(2,1)S(1)} %bitcast.22, bf16[128,3072]{1,0:T(8,128)(2,1)S(1)} %bitcast.15, ...), custom_call_target="tpu_custom_call" | custom-call | tf_op jit(solution)/shard_map/pallas_call | solution.py:380
  131.5 1.9 %collective-permute-start.2 = (bf16[2,48,3072]{2,1,0:T(8,128)(2,1)S(1)}, bf16[2,48,3072]{2,1,0:T(8,128)(2,1)S(1)}, u32[]{:S(2)}, u32[]{:S(2)}) collective-permute-start(bf16[2,48,3072]{2,1,0:T(8,128)(2,1)S(1)} %get-tuple-element.29), channel_id=1, source_target_pairs={{0,1},{1,2},{2,3},{3,4},{4,5},{5,6},{6,7},{7,8},{8,9},{9,10},{10,1... | collective-permute-start | bytes 1769480 | tf_op jit(solution)/shard_map/ppermute | solution.py:388
  133.4 6.0 %collective-permute-start.3 = (bf16[2,48,3072]{2,1,0:T(8,128)(2,1)S(1)}, bf16[2,48,3072]{2,1,0:T(8,128)(2,1)S(1)}, u32[]{:S(2)}, u32[]{:S(2)}) collective-permute-start(bf16[2,48,3072]{2,1,0:T(8,128)(2,1)S(1)} %get-tuple-element.30), channel_id=1, source_target_pairs={{1,0},{2,1},{3,2},{4,3},{5,4},{6,5},{7,6},{8,7},{9,8},{10,9},{11,1... | collective-permute-start | bytes 1769480 | tf_op jit(solution)/shard_map/ppermute | solution.py:387
  139.4 7.4 %collective-permute-done.2.from_low_ref = bf16[2,48,3072]{2,1,0:T(8,128)(2,1)S(1)} collective-permute-done((bf16[2,48,3072]{2,1,0:T(8,128)(2,1)S(1)}, bf16[2,48,3072]{2,1,0:T(8,128)(2,1)S(1)}, u32[]{:S(2)}, u32[]{:S(2)}) %collective-permute-start.2) | collective-permute-done | bytes 589856 | tf_op jit(solution)/shard_map/ppermute | solution.py:388
  146.8 1.6 collective-permute-done.3.from_high_ref
  148.4 2.1 %shard_map.81 = (f32[128,3072]{1,0:T(8,128)}, bf16[128,3072]{1,0:T(8,128)(2,1)}) custom-call(f32[128,3072]{1,0:T(8,128)S(1)} %get-tuple-element.27.ks_ref, f32[128,3072]{1,0:T(8,128)S(1)} %get-tuple-element.28.vs_ref, bf16[2,48,3072]{2,1,0:T(8,128)(2,1)S(1)} %collective-permute-done.2.from_low_ref, bf16[2,48,3072]{2,1,0:T(8,128)(2,1)S(1)} %collective-permute-done.3.from_high_ref), custom_call_target="tpu_custom_call" | custom-call | tf_op jit(solution)/shard_map/pallas_call | solution.py:391
  150.5 29.3 %all-to-all-done.2.back_ref = bf16[16,8,9216]{2,1,0:T(8,128)(2,1)} async-done(((bf16[16,8,9216]{2,1,0:T(8,128)(2,1)}), bf16[16,8,9216]{2,1,0:T(8,128)(2,1)}, u32[]{:S(2)}, u32[]{:S(2)}) %all-to-all-start.2) | async-done | bytes 2359328 | tf_op jit(solution)/shard_map/all_to_all | solution.py:275
  179.7 4.0 %shard_map.82 = (bf16[128,3072]{1,0:T(8,128)(2,1)}, bf16[128,3072]{1,0:T(8,128)(2,1)}, bf16[128,3072]{1,0:T(8,128)(2,1)}) custom-call(bf16[16,8,9216]{2,1,0:T(8,128)(2,1)} %all-to-all-done.2.back_ref, f32[128,3072]{1,0:T(8,128)} %get-tuple-element.26.qs_ref, f32[128,3072]{1,0:T(8,128)} %get-tuple-element.31.ks_ref), custom_call_target="tpu_custom_call" | custom-call | tf_op jit(solution)/shard_map/pallas_call | solution.py:399
Async XLA Ops:
  3.4 64.6 %all-to-all-start = ((bf16[16,8,9216]{2,1,0:T(8,128)(2,1)}), bf16[16,8,9216]{2,1,0:T(8,128)(2,1)S(1)}, u32[]{:S(2)}, u32[]{:S(2)}) async-start(bf16[16,8,9216]{2,1,0:T(8,128)(2,1)} %shard_map.75), calls=%async_computation | async-start | bytes 4718592 | tf_op jit(solution)/shard_map/all_to_all | solution.py:275
  13.0 21.5 %copy-start = (bf16[1,8,16,3072]{3,2,1,0:T(8,128)(2,1)S(1)}, bf16[1,8,16,3072]{3,2,1,0:T(8,128)(2,1)}, u32[]{:S(2)}) copy-start(bf16[1,8,16,3072]{3,2,1,0:T(8,128)(2,1)} %param.5) | copy-start | bytes 2359300
  16.3 18.2 %collective-permute-start = (bf16[2,48,3072]{2,1,0:T(8,128)(2,1)}, bf16[2,48,3072]{2,1,0:T(8,128)(2,1)}, u32[]{:S(2)}, u32[]{:S(2)}) collective-permute-start(bf16[2,48,3072]{2,1,0:T(8,128)(2,1)} %get-tuple-element.20), channel_id=1, source_target_pairs={{0,1},{1,2},{2,3},{3,4},{4,5},{5,6},{6,7},{7,8},{8,9},{9,10},{10,1... | collective-permute-start | bytes 1769480 | tf_op jit(solution)/shard_map/ppermute | solution.py:317
  18.2 16.3 %collective-permute-start.1 = (bf16[2,48,3072]{2,1,0:T(8,128)(2,1)}, bf16[2,48,3072]{2,1,0:T(8,128)(2,1)}, u32[]{:S(2)}, u32[]{:S(2)}) collective-permute-start(bf16[2,48,3072]{2,1,0:T(8,128)(2,1)} %get-tuple-element.21), channel_id=1, source_target_pairs={{1,0},{2,1},{3,2},{4,3},{5,4},{6,5},{7,6},{8,7},{9,8},{10,9},{11,1... | collective-permute-start | bytes 1769480 | tf_op jit(solution)/shard_map/ppermute | solution.py:318
  34.5 1.1 copy-start.1
  35.6 1.1 copy-start.3
  119.4 5.0 %copy-start.2 = (bf16[1,8,16,3072]{3,2,1,0:T(8,128)(2,1)S(1)}, bf16[1,8,16,3072]{3,2,1,0:T(8,128)(2,1)}, u32[]{:S(2)}) copy-start(bf16[1,8,16,3072]{3,2,1,0:T(8,128)(2,1)} %param.6) | copy-start | bytes 2359300
  119.4 5.0 %copy-start.4 = (bf16[1,8,16,3072]{3,2,1,0:T(8,128)(2,1)S(1)}, bf16[1,8,16,3072]{3,2,1,0:T(8,128)(2,1)}, u32[]{:S(2)}) copy-start(bf16[1,8,16,3072]{3,2,1,0:T(8,128)(2,1)} %param.4) | copy-start | bytes 2359300
  119.4 60.4 %all-to-all-start.2 = ((bf16[16,8,9216]{2,1,0:T(8,128)(2,1)}), bf16[16,8,9216]{2,1,0:T(8,128)(2,1)}, u32[]{:S(2)}, u32[]{:S(2)}) async-start(bf16[16,8,9216]{2,1,0:T(8,128)(2,1)} %shard_map.79), calls=%async_computation.2 | async-start | bytes 4718592 | tf_op jit(solution)/shard_map/all_to_all | solution.py:275
  131.5 15.3 %collective-permute-start.2 = (bf16[2,48,3072]{2,1,0:T(8,128)(2,1)S(1)}, bf16[2,48,3072]{2,1,0:T(8,128)(2,1)S(1)}, u32[]{:S(2)}, u32[]{:S(2)}) collective-permute-start(bf16[2,48,3072]{2,1,0:T(8,128)(2,1)S(1)} %get-tuple-element.29), channel_id=1, source_target_pairs={{0,1},{1,2},{2,3},{3,4},{4,5},{5,6},{6,7},{7,8},{8,9},{9,10},{10,1... | collective-permute-start | bytes 1769480 | tf_op jit(solution)/shard_map/ppermute | solution.py:388
  133.4 15.0 %collective-permute-start.3 = (bf16[2,48,3072]{2,1,0:T(8,128)(2,1)S(1)}, bf16[2,48,3072]{2,1,0:T(8,128)(2,1)S(1)}, u32[]{:S(2)}, u32[]{:S(2)}) collective-permute-start(bf16[2,48,3072]{2,1,0:T(8,128)(2,1)S(1)} %get-tuple-element.30), channel_id=1, source_target_pairs={{1,0},{2,1},{3,2},{4,3},{5,4},{6,5},{7,6},{8,7},{9,8},{10,9},{11,1... | collective-permute-start | bytes 1769480 | tf_op jit(solution)/shard_map/ppermute | solution.py:387

commit v2 on v1

--- a/solution.py
+++ b/solution.py
@@ -16,7 +16,6 @@
 F32 = jnp.float32
 
 FWD_HEADS = 4
-SCORE_HEADS = 8
 TIME_HEADS = 8
 BWD_HEADS = 4
 RIM_HEADS = 8
@@ -137,7 +136,8 @@
             to_high_ref[half, :, at] = wide[head][rim + queries :].astype(BF16)
     for head in heads:
         key = window_of(k_ref, low_ref, high_ref, 0, head)
-        qs_ref[:, lanes(head)] = dot(score_grads[head], key, TN) * SCALING
+        query_sum = dot(score_grads[head], key, TN) * SCALING
+        qs_ref[:, :, lanes(head)] = chunked(query_sum, qs_ref.shape[0]).astype(BF16)
 
 
 def same_position(rows, spots):
@@ -146,39 +146,75 @@
     return left % spots == right % spots
 
 
-def temporal_scores_kernel(q_ref, k_ref, g_ref, sent_ref, grad_ref, probs_ref):
-    del sent_ref
-    frames, spots = q_ref.shape[0], q_ref.shape[1]
+def temporal_scores_kernel(moved_ref, begun_ref, sent_ref, probs_ref, held, sems):
+    del begun_ref
+    frames, spots = moved_ref.shape[0], moved_ref.shape[1]
+    channels = HEADS * HEAD_DIM
     same = same_position(frames * spots, spots)
-    heads = range(q_ref.shape[2] // HEAD_DIM)
-    scores = [dot(head_rows(k_ref, head), head_rows(q_ref, head), NT) for head in heads]
-    probs = [softmax_columns(jnp.where(same, part, NEG_FILL)) for part in scores]
-    grads = [dot(probs[head].astype(BF16), head_rows(g_ref, head), NN) for head in heads]
-    for head in heads:
-        probs_ref[head] = probs[head]
-    for head in heads:
-        grad_ref[:, :, lanes(head)] = chunked(grads[head], frames).astype(BF16)
-
-
-def temporal_grads_kernel(q_ref, k_ref, g_ref, s_ref, probs_ref, out_ref):
-    frames = q_ref.shape[0]
-    width = q_ref.shape[2]
-    heads = range(width // HEAD_DIM)
-    spatial = [head_rows(s_ref, head) for head in heads]
-    prob_grads = [dot(spatial[head], head_rows(g_ref, head), NT) for head in heads]
-    outs = [dot(probs_ref[head].astype(BF16), spatial[head], TN) for head in heads]
-    score_grads = []
-    for head in heads:
-        probs = probs_ref[head]
-        weights = probs.astype(BF16).astype(F32)
-        grad_dot = jnp.sum(weights * prob_grads[head], 0, keepdims=True)
-        score_grads.append((probs * (prob_grads[head] - grad_dot)).astype(BF16))
-    query_parts = [dot(score_grads[head], head_rows(k_ref, head), TN) * SCALING for head in heads]
-    key_parts = [dot(score_grads[head], head_rows(q_ref, head), NN) * SCALING for head in heads]
-    for place, parts in enumerate((outs, query_parts, key_parts)):
-        for head in heads:
-            first = place * width + head * HEAD_DIM
-            out_ref[:, :, first : first + HEAD_DIM] = chunked(parts[head], frames).astype(BF16)
+    stores = []
+    for group in range(HEADS // TIME_HEADS):
+        heads = range(group * TIME_HEADS, (group + 1) * TIME_HEADS)
+        scores = [
+            dot(head_rows(moved_ref, HEADS + head), head_rows(moved_ref, head), NT) for head in heads
+        ]
+        probs = [softmax_columns(jnp.where(same, part, NEG_FILL)) for part in scores]
+        grads = [
+            dot(part.astype(BF16), head_rows(moved_ref, 2 * HEADS + head), NN)
+            for part, head in zip(probs, heads)
+        ]
+        for part, head in zip(probs, heads):
+            probs_ref[head] = part
+        for part, head in zip(grads, heads):
+            held[:, :, lanes(head)] = chunked(part, frames).astype(BF16)
+        first, last = group * TIME_HEADS * HEAD_DIM, (group + 1) * TIME_HEADS * HEAD_DIM
+        stores.append(
+            started(
+                held.at[:, :, first:last],
+                sent_ref.at[:, :, channels + first : channels + last],
+                sems.at[group],
+            )
+        )
+    for store in stores:
+        store.wait()
+
+
+def temporal_grads_kernel(moved_ref, both_ref, probs_ref, out_ref, spatial_held, held, load_sems, store_sems):
+    frames = moved_ref.shape[0]
+    width = TIME_HEADS * HEAD_DIM
+    groups = range(HEADS // TIME_HEADS)
+    loads, stores = [], []
+    for group in groups:
+        at = slice(group * width, (group + 1) * width)
+        loads.append(started(both_ref.at[:, :, at], spatial_held.at[:, :, at], load_sems.at[group]))
+    for group in groups:
+        heads = range(group * TIME_HEADS, (group + 1) * TIME_HEADS)
+        loads[group].wait()
+        spatial = [head_rows(spatial_held, head) for head in heads]
+        prob_grads = [
+            dot(part, head_rows(moved_ref, 2 * HEADS + head), NT) for part, head in zip(spatial, heads)
+        ]
+        outs = [dot(probs_ref[head].astype(BF16), part, TN) for part, head in zip(spatial, heads)]
+        score_grads = []
+        for prob_grad, head in zip(prob_grads, heads):
+            probs = probs_ref[head]
+            weights = probs.astype(BF16).astype(F32)
+            grad_dot = jnp.sum(weights * prob_grad, 0, keepdims=True)
+            score_grads.append((probs * (prob_grad - grad_dot)).astype(BF16))
+        query_parts = [
+            dot(part, head_rows(moved_ref, HEADS + head), TN) * SCALING
+            for part, head in zip(score_grads, heads)
+        ]
+        key_parts = [
+            dot(part, head_rows(moved_ref, head), NN) * SCALING for part, head in zip(score_grads, heads)
+        ]
+        for place, parts in enumerate((outs, query_parts, key_parts)):
+            for step, part in enumerate(parts):
+                first = (group * 3 + place) * width + step * HEAD_DIM
+                held[:, :, first : first + HEAD_DIM] = chunked(part, frames).astype(BF16)
+        at = slice(group * 3 * width, (group + 1) * 3 * width)
+        stores.append(started(held.at[:, :, at], out_ref.at[:, :, at], store_sems.at[group]))
+    for store in stores:
+        store.wait()
 
 
 def rims_kernel(k_first_ref, v_first_ref, k_last_ref, v_last_ref, to_low_ref, to_high_ref):
@@ -224,44 +260,61 @@
 def rim_add_kernel(ks_ref, vs_ref, from_low_ref, from_high_ref, key_ref, value_ref):
     rim = from_low_ref.shape[1]
     rows = ks_ref.shape[0]
-    for half, (sum_ref, out_ref) in enumerate(((ks_ref, key_ref), (vs_ref, value_ref))):
-        out_ref[:rim] = (sum_ref[:rim] + from_low_ref[half].astype(F32)).astype(out_ref.dtype)
-        out_ref[rim : rows - rim] = sum_ref[rim : rows - rim].astype(out_ref.dtype)
-        out_ref[rows - rim :] = (sum_ref[rows - rim :] + from_high_ref[half].astype(F32)).astype(
-            out_ref.dtype
+    totals = [
+        jnp.concatenate(
+            [
+                sum_ref[:rim] + from_low_ref[half].astype(F32),
+                sum_ref[rim : rows - rim],
+                sum_ref[rows - rim :] + from_high_ref[half].astype(F32),
+            ],
+            0,
         )
+        for half, sum_ref in enumerate((ks_ref, vs_ref))
+    ]
+    key_ref[...] = chunked(totals[0], key_ref.shape[0]).astype(BF16)
+    value_ref[...] = totals[1].astype(BF16)
 
 
 def last_sum_kernel(back_ref, qs_ref, ks_ref, *refs):
-    outs, (back, qs, ks), results, (load_sems, store_sems) = refs[:3], refs[3:6], refs[6:9], refs[9:]
+    outs, (back, qs, ks), results, (load_sems, store_sems) = refs[:3], refs[3:6], refs[6:8], refs[8:]
     pieces = load_sems.shape[0]
-    chunks, rows = back.shape[0] // pieces, qs.shape[0] // pieces
+    chunks = back.shape[0] // pieces
     width = TIME_HEADS * HEAD_DIM
+    groups = range(HEADS // TIME_HEADS)
+    pairs = ((back_ref, back), (qs_ref, qs), (ks_ref, ks))
+    somes = [slice(piece * chunks, (piece + 1) * chunks) for piece in range(pieces)]
     loads, stores = [], []
-    for piece in range(pieces):
-        some = slice(piece * chunks, (piece + 1) * chunks)
-        at = slice(piece * rows, (piece + 1) * rows)
-        pairs = ((back_ref.at[some], back.at[some]), (qs_ref.at[at], qs.at[at]), (ks_ref.at[at], ks.at[at]))
+    for piece, some in enumerate(somes):
         loads.append(
-            [started(*pair, load_sems.at[piece, place]) for place, pair in enumerate(pairs)]
+            [
+                started(source.at[some], target.at[some], load_sems.at[piece, place])
+                for place, (source, target) in enumerate(pairs)
+            ]
         )
-    for piece in range(pieces):
+    for piece, some in enumerate(somes):
         for load in loads[piece]:
             load.wait()
-        some = slice(piece * chunks, (piece + 1) * chunks)
-        at = slice(piece * rows, (piece + 1) * rows)
-        for group in range(HEADS // TIME_HEADS):
+        for group in groups:
             to = slice(group * width, (group + 1) * width)
-            parts = [
-                flat_rows(back[some, :, (group * 3 + place) * width : (group * 3 + place + 1) * width])
-                for place in range(3)
-            ]
-            results[0][at, to] = parts[0].astype(BF16)
-            results[1][at, to] = (parts[1] + qs[at, to]).astype(BF16)
-            results[2][at, to] = (parts[2] + ks[at, to]).astype(BF16)
-        for place in range(3):
+            first = group * 3 * width
             stores.append(
-                started(results[place].at[at], outs[place].at[at], store_sems.at[piece, place])
+                started(
+                    back.at[some, :, first : first + width],
+                    outs[0].at[some, :, to],
+                    store_sems.at[piece, group],
+                )
+            )
+            for place, (kept, result) in enumerate(((qs, results[0]), (ks, results[1]))):
+                first += width
+                part = back[some, :, first : first + width].astype(F32)
+                result[some, :, to] = (part + kept[some, :, to].astype(F32)).astype(BF16)
+        for place in range(2):
+            stores.append(
+                started(
+                    results[place].at[some],
+                    outs[1 + place].at[some],
+                    store_sems.at[piece, len(groups) + place],
+                )
             )
     for store in stores:
         store.wait()
@@ -269,6 +322,10 @@
 
 def in_hbm(tensor):
     return pltpu.with_memory_space_constraint(tensor, pltpu.HBM)
+
+
+def in_vmem(tensor):
+    return pltpu.with_memory_space_constraint(tensor, pltpu.VMEM)
 
 
 def exchange(chunks):
@@ -341,36 +398,36 @@
         pltpu.HBM((parts, spots, 2 * channels), BF16),
     )(first_row, query, key, value, low, high)
 
-    count = HEADS // SCORE_HEADS
-    sent, probs = call(
+    moved = in_vmem(moved)
+    groups = HEADS // TIME_HEADS
+    in_place = pl.BlockSpec(memory_space=pltpu.VMEM)
+    sent, probs = pl.pallas_call(
         temporal_scores_kernel,
-        count,
-        [chunk_block(SCORE_HEADS, place * count) for place in range(3)]
-        + [anywhere],
-        [
-            chunk_block(SCORE_HEADS, count),
-            pl.BlockSpec((SCORE_HEADS, tokens, tokens), lambda i: (i, 0, 0)),
+        in_specs=[in_place, anywhere],
+        out_specs=[anywhere, in_place],
+        out_shape=[pltpu.HBM(sent.shape, BF16), pltpu.VMEM((HEADS, tokens, tokens), F32)],
+        scratch_shapes=[
+            pltpu.VMEM((parts, spots, channels), BF16),
+            pltpu.SemaphoreType.DMA((groups,)),
         ],
-        [
-            pltpu.HBM(sent.shape, BF16),
-            jax.ShapeDtypeStruct((HEADS, tokens, tokens), F32),
+        input_output_aliases={1: 0},
+        compiler_params=params,
+    )(moved, in_hbm(sent))
+    both = in_hbm(exchange(sent))
+
+    parts_out = pl.pallas_call(
+        temporal_grads_kernel,
+        in_specs=[in_place, anywhere, in_place],
+        out_specs=anywhere,
+        out_shape=pltpu.HBM(joined_shape, BF16),
+        scratch_shapes=[
+            pltpu.VMEM((parts, spots, channels), BF16),
+            pltpu.VMEM(joined_shape, BF16),
+            pltpu.SemaphoreType.DMA((groups,)),
+            pltpu.SemaphoreType.DMA((groups,)),
         ],
-        input_output_aliases={3: 0},
-    )(moved, moved, moved, sent)
-    both = in_hbm(exchange(sent))
-
-    count = HEADS // TIME_HEADS
-    parts_out = call(
-        temporal_grads_kernel,
-        count,
-        [chunk_block(TIME_HEADS, place * count) for place in range(3)]
-        + [
-            chunk_block(TIME_HEADS, 0),
-            pl.BlockSpec((TIME_HEADS, tokens, tokens), lambda i: (i, 0, 0)),
-        ],
-        chunk_block(3 * TIME_HEADS, 0),
-        pltpu.HBM((parts, spots, 3 * channels), BF16),
-    )(moved, moved, moved, both, probs)
+        compiler_params=params,
+    )(moved, both, in_vmem(probs))
     parts_out, both = lax.optimization_barrier((parts_out, both))
     back = exchange(parts_out)
 
@@ -381,8 +438,8 @@
         functools.partial(spatial_bwd_kernel, total_rows, breadth),
         count,
         [scalar, own, own, own, rims_block(BWD_HEADS), rims_block(BWD_HEADS), chunk_block(BWD_HEADS, count)],
-        [own, own, own, rims_block(BWD_HEADS), rims_block(BWD_HEADS)],
-        [pltpu.HBM((tokens, channels), F32), whole, whole, rims, rims],
+        [chunk_block(BWD_HEADS, 0), own, own, rims_block(BWD_HEADS), rims_block(BWD_HEADS)],
+        [pltpu.HBM((parts, spots, channels), BF16), whole, whole, rims, rims],
     )(first_row, query, key, value, low, high, in_hbm(both))
     from_high = lax.ppermute(to_low, "rows", downward)
     from_low = lax.ppermute(to_high, "rows", upward)
@@ -392,19 +449,18 @@
         rim_add_kernel,
         HEADS // RIM_HEADS,
         [own, own, rims_block(RIM_HEADS), rims_block(RIM_HEADS)],
-        [own, own],
-        [pltpu.HBM((tokens, channels), F32), final],
+        [chunk_block(RIM_HEADS, 0), own],
+        [pltpu.HBM((parts, spots, channels), BF16), final],
     )(ks, vs, from_low, from_high)
 
     temporal_out, query_grad, key_grad = pl.pallas_call(
         last_sum_kernel,
         in_specs=[anywhere] * 3,
         out_specs=[anywhere] * 3,
-        out_shape=[pltpu.HBM((tokens, channels), BF16)] * 3,
+        out_shape=[pltpu.HBM((parts, spots, channels), BF16)] * 3,
         scratch_shapes=[pltpu.VMEM(joined_shape, BF16)]
-        + [pltpu.VMEM((tokens, channels), F32)] * 2
-        + [pltpu.VMEM((tokens, channels), BF16)] * 3
-        + [pltpu.SemaphoreType.DMA((PIECES, 3))] * 2,
+        + [pltpu.VMEM((parts, spots, channels), BF16)] * 4
+        + [pltpu.SemaphoreType.DMA((PIECES, 3)), pltpu.SemaphoreType.DMA((PIECES, groups + 2))],
         compiler_params=params,
     )(back, in_hbm(qs), in_hbm(ks))
     return tuple(

time: 185 us -> 182 us (0.984)
  Pallas kernels: 32.5 us -> 30.3 us
where the time goes in v2:
time: 182 us
  waiting for transfers between devices  73.4 us (40%)
  blocking collectives  44.3 us (24%)
  starting transfers between devices  30.5 us (17%)
  Pallas kernels  30.3 us (17%)
  local copies, waits for them, and re-layouts  2.28 us (1%)
    all_to_all x2, waiting for transfers between devices, exchange(): return lax.all_to_all(chunks, 'tm', split_axis=0, concat_axis=0, tiled=True)  54.3 us
    all_to_all x1, blocking collectives, exchange(): return lax.all_to_all(chunks, 'tm', split_axis=0, concat_axis=0, tiled=True)  44.3 us
    all_to_all x2, starting transfers between devices, exchange(): return lax.all_to_all(chunks, 'tm', split_axis=0, concat_axis=0, tiled=True)  14.6 us
    ppermute x1, waiting for transfers between devices, on_device(): low = lax.ppermute(to_high, 'rows', upward)  10.2 us
    ppermute x1, waiting for transfers between devices, on_device(): from_low = lax.ppermute(to_high, 'rows', upward)  7.38 us
    pallas_call x1, Pallas kernels, on_device(): call(functools.partial(spatial_bwd_kernel, total_rows, breadth), count, [...  7.04 us
    pallas_call x1, Pallas kernels, on_device(): call(functools.partial(spatial_fwd_kernel, total_rows, breadth), HEADS //...  6.17 us
    ppermute x1, starting transfers between devices, on_device(): high = lax.ppermute(to_low, 'rows', downward)  6.05 us
  transfers between devices with their start and end apart: 6, of which 5 were waited for; matrix products, arithmetic and copies ran while one was open for 0% of the time, Pallas kernels for 10%

profile of v2, /device:TPU:6, one launch (start us, length us, event | category | flops | bytes accessed | tf_op | source)
XLA Modules:
  0.0 181.5 jit_solution(13641356210892447624)
XLA Ops:
  0.6 2.7 %shard_map.75 = bf16[16,8,9216]{2,1,0:T(8,128)(2,1)} custom-call(bf16[16,8,3072]{2,1,0:T(8,128)(2,1)} %bitcast.20, bf16[16,8,3072]{2,1,0:T(8,128)(2,1)} %bitcast.11, bf16[16,8,3072]{2,1,0:T(8,128)(2,1)} %bitcast.23), custom_call_target="tpu_custom_call" | custom-call | tf_op jit(solution)/shard_map/pallas_call | solution.py:378
  3.4 9.6 %all-to-all-start = ((bf16[16,8,9216]{2,1,0:T(8,128)(2,1)}), bf16[16,8,9216]{2,1,0:T(8,128)(2,1)S(1)}, u32[]{:S(2)}, u32[]{:S(2)}) async-start(bf16[16,8,9216]{2,1,0:T(8,128)(2,1)} %shard_map.75), calls=%async_computation | async-start | bytes 4718592 | tf_op jit(solution)/shard_map/all_to_all | solution.py:332
  13.0 0.0 copy-start
  13.0 3.3 %shard_map.76 = (bf16[2,48,3072]{2,1,0:T(8,128)(2,1)}, bf16[2,48,3072]{2,1,0:T(8,128)(2,1)}) custom-call(bf16[128,3072]{1,0:T(8,128)(2,1)} %bitcast.12, bf16[128,3072]{1,0:T(8,128)(2,1)} %bitcast.16, bf16[128,3072]{1,0:T(8,128)(2,1)} %bitcast.13, bf16[128,3072]{1,0:T(8,128)(2,1)} %bitcast.17), custom_call_target="tpu_custom_call" | custom-call | tf_op jit(solution)/shard_map/pallas_call | solution.py:367
  16.3 1.9 %collective-permute-start = (bf16[2,48,3072]{2,1,0:T(8,128)(2,1)}, bf16[2,48,3072]{2,1,0:T(8,128)(2,1)}, u32[]{:S(2)}, u32[]{:S(2)}) collective-permute-start(bf16[2,48,3072]{2,1,0:T(8,128)(2,1)} %get-tuple-element.20), channel_id=1, source_target_pairs={{0,1},{1,2},{2,3},{3,4},{4,5},{5,6},{6,7},{7,8},{8,9},{9,10},{10,1... | collective-permute-start | bytes 1769480 | tf_op jit(solution)/shard_map/ppermute | solution.py:374
  18.2 6.0 %collective-permute-start.1 = (bf16[2,48,3072]{2,1,0:T(8,128)(2,1)}, bf16[2,48,3072]{2,1,0:T(8,128)(2,1)}, u32[]{:S(2)}, u32[]{:S(2)}) collective-permute-start(bf16[2,48,3072]{2,1,0:T(8,128)(2,1)} %get-tuple-element.21), channel_id=1, source_target_pairs={{1,0},{2,1},{3,2},{4,3},{5,4},{6,5},{7,6},{8,7},{9,8},{10,9},{11,1... | collective-permute-start | bytes 1769480 | tf_op jit(solution)/shard_map/ppermute | solution.py:375
  24.2 10.2 %collective-permute-done.low_ref = bf16[2,48,3072]{2,1,0:T(8,128)(2,1)} collective-permute-done((bf16[2,48,3072]{2,1,0:T(8,128)(2,1)}, bf16[2,48,3072]{2,1,0:T(8,128)(2,1)}, u32[]{:S(2)}, u32[]{:S(2)}) %collective-permute-start) | collective-permute-done | bytes 589856 | tf_op jit(solution)/shard_map/ppermute | solution.py:374
  34.5 0.0 collective-permute-done.1.high_ref
  34.5 0.0 copy-done
  34.5 0.0 copy-start.1
  34.5 1.1 copy-done.1
  35.6 0.0 copy-start.3
  35.6 1.1 copy-done.3
  36.7 6.2 %shard_map.77.begun_ref = bf16[16,8,6144]{2,1,0:T(8,128)(2,1)} custom-call(s32[1]{0:T(128)} %bitcast.3.first_ref, bf16[128,3072]{1,0:T(8,128)(2,1)S(1)} %bitcast.21, bf16[128,3072]{1,0:T(8,128)(2,1)S(1)} %bitcast.14, bf16[128,3072]{1,0:T(8,128)(2,1)S(1)} %bitcast.18, bf16[2,48,3072]{2,1,0:T(8,128)(2,1)} %collective-permute-done.low_ref, ...), custom_call_target="tpu_custom_call" | custom-call | tf_op jit(solution)/shard_map/pallas_call | solution.py:393
  42.9 25.0 %all-to-all-done.moved_ref = bf16[16,8,9216]{2,1,0:T(8,128)(2,1)S(1)} async-done(((bf16[16,8,9216]{2,1,0:T(8,128)(2,1)}), bf16[16,8,9216]{2,1,0:T(8,128)(2,1)S(1)}, u32[]{:S(2)}, u32[]{:S(2)}) %all-to-all-start) | async-done | bytes 2359328 | tf_op jit(solution)/shard_map/all_to_all | solution.py:332
  67.9 2.1 %shard_map.78 = (bf16[16,8,6144]{2,1,0:T(8,128)(2,1)}, f32[24,128,128]{2,1,0:T(8,128)S(1)}) custom-call(bf16[16,8,9216]{2,1,0:T(8,128)(2,1)S(1)} %all-to-all-done.moved_ref, bf16[16,8,6144]{2,1,0:T(8,128)(2,1)} %shard_map.77.begun_ref), custom_call_target="tpu_custom_call", output_to_operand_aliasing={{0}: (1, {})} | custom-call | tf_op jit(solution)/shard_map/pallas_call | solution.py:404
  70.1 44.3 %all_to_all.15.both_ref.g_ref = bf16[16,8,6144]{2,1,0:T(8,128)(2,1)} all-to-all(bf16[16,8,6144]{2,1,0:T(8,128)(2,1)} %get-tuple-element.22), channel_id=1, replica_groups=mesh['tm'=16,'rows'=16] {'tm'}, dimensions={0} | all-to-all | bytes 3145728 | tf_op jit(solution)/shard_map/all_to_all | solution.py:332
  114.4 3.8 %shard_map.79 = bf16[16,8,9216]{2,1,0:T(8,128)(2,1)} custom-call(bf16[16,8,9216]{2,1,0:T(8,128)(2,1)S(1)} %all-to-all-done.moved_ref, bf16[16,8,6144]{2,1,0:T(8,128)(2,1)} %all_to_all.15.both_ref.g_ref, f32[24,128,128]{2,1,0:T(8,128)S(1)} %get-tuple-element.23.probs_ref), custom_call_target="tpu_custom_call" | custom-call | tf_op jit(solution)/shard_map/pallas_call | solution.py:418
  118.2 0.0 copy-start.2
  118.2 0.0 copy-start.4
  118.2 5.0 %all-to-all-start.2 = ((bf16[16,8,9216]{2,1,0:T(8,128)(2,1)}), bf16[16,8,9216]{2,1,0:T(8,128)(2,1)}, u32[]{:S(2)}, u32[]{:S(2)}) async-start(bf16[16,8,9216]{2,1,0:T(8,128)(2,1)} %shard_map.79), calls=%async_computation.2 | async-start | bytes 4718592 | tf_op jit(solution)/shard_map/all_to_all | solution.py:332
  123.3 0.0 copy-done.2
  123.3 0.0 copy-done.4
  123.3 7.0 %shard_map.80 = (bf16[16,8,3072]{2,1,0:T(8,128)(2,1)}, f32[128,3072]{1,0:T(8,128)S(1)}, f32[128,3072]{1,0:T(8,128)S(1)}, bf16[2,48,3072]{2,1,0:T(8,128)(2,1)S(1)}, bf16[2,48,3072]{2,1,0:T(8,128)(2,1)S(1)}) custom-call(s32[1]{0:T(128)} %bitcast.3.first_ref, bf16[128,3072]{1,0:T(8,128)(2,1)S(1)} %bitcast.22, bf16[128,3072]{1,0:T(8,128)(2,1)S(1)} %bitcast.15, ...), custom_call_target="tpu_custom_call" | custom-call | tf_op jit(solution)/shard_map/pallas_call | solution.py:437
  130.3 1.9 %collective-permute-start.2 = (bf16[2,48,3072]{2,1,0:T(8,128)(2,1)S(1)}, bf16[2,48,3072]{2,1,0:T(8,128)(2,1)S(1)}, u32[]{:S(2)}, u32[]{:S(2)}) collective-permute-start(bf16[2,48,3072]{2,1,0:T(8,128)(2,1)S(1)} %get-tuple-element.29), channel_id=1, source_target_pairs={{0,1},{1,2},{2,3},{3,4},{4,5},{5,6},{6,7},{7,8},{8,9},{9,10},{10,1... | collective-permute-start | bytes 1769480 | tf_op jit(solution)/shard_map/ppermute | solution.py:445
  132.2 6.0 %collective-permute-start.3 = (bf16[2,48,3072]{2,1,0:T(8,128)(2,1)S(1)}, bf16[2,48,3072]{2,1,0:T(8,128)(2,1)S(1)}, u32[]{:S(2)}, u32[]{:S(2)}) collective-permute-start(bf16[2,48,3072]{2,1,0:T(8,128)(2,1)S(1)} %get-tuple-element.30), channel_id=1, source_target_pairs={{1,0},{2,1},{3,2},{4,3},{5,4},{6,5},{7,6},{8,7},{9,8},{10,9},{11,1... | collective-permute-start | bytes 1769480 | tf_op jit(solution)/shard_map/ppermute | solution.py:444
  138.3 7.4 %collective-permute-done.2.from_low_ref = bf16[2,48,3072]{2,1,0:T(8,128)(2,1)S(1)} collective-permute-done((bf16[2,48,3072]{2,1,0:T(8,128)(2,1)S(1)}, bf16[2,48,3072]{2,1,0:T(8,128)(2,1)S(1)}, u32[]{:S(2)}, u32[]{:S(2)}) %collective-permute-start.2) | collective-permute-done | bytes 589856 | tf_op jit(solution)/shard_map/ppermute | solution.py:445
  145.7 1.6 collective-permute-done.3.from_high_ref
  147.2 1.9 %shard_map.81 = (bf16[16,8,3072]{2,1,0:T(8,128)(2,1)}, bf16[128,3072]{1,0:T(8,128)(2,1)}) custom-call(f32[128,3072]{1,0:T(8,128)S(1)} %get-tuple-element.27.ks_ref, f32[128,3072]{1,0:T(8,128)S(1)} %get-tuple-element.28.vs_ref, bf16[2,48,3072]{2,1,0:T(8,128)(2,1)S(1)} %collective-permute-done.2.from_low_ref, ...), custom_call_target="tpu_custom_call" | custom-call | tf_op jit(solution)/shard_map/pallas_call | solution.py:448
  149.2 29.2 %all-to-all-done.2.back_ref = bf16[16,8,9216]{2,1,0:T(8,128)(2,1)} async-done(((bf16[16,8,9216]{2,1,0:T(8,128)(2,1)}), bf16[16,8,9216]{2,1,0:T(8,128)(2,1)}, u32[]{:S(2)}, u32[]{:S(2)}) %all-to-all-start.2) | async-done | bytes 2359328 | tf_op jit(solution)/shard_map/all_to_all | solution.py:332
  178.4 3.1 %shard_map.82 = (bf16[16,8,3072]{2,1,0:T(8,128)(2,1)}, bf16[16,8,3072]{2,1,0:T(8,128)(2,1)}, bf16[16,8,3072]{2,1,0:T(8,128)(2,1)}) custom-call(bf16[16,8,9216]{2,1,0:T(8,128)(2,1)} %all-to-all-done.2.back_ref, bf16[16,8,3072]{2,1,0:T(8,128)(2,1)} %get-tuple-element.26.qs_ref, bf16[16,8,3072]{2,1,0:T(8,128)(2,1)} %get-tuple-element.31.ks_ref), custom_call_target="tpu_custom_call" | custom-call | tf_op jit(solution)/shard_map/pallas_call | solution.py:456
Async XLA Ops:
  3.4 64.6 %all-to-all-start = ((bf16[16,8,9216]{2,1,0:T(8,128)(2,1)}), bf16[16,8,9216]{2,1,0:T(8,128)(2,1)S(1)}, u32[]{:S(2)}, u32[]{:S(2)}) async-start(bf16[16,8,9216]{2,1,0:T(8,128)(2,1)} %shard_map.75), calls=%async_computation | async-start | bytes 4718592 | tf_op jit(solution)/shard_map/all_to_all | solution.py:332
  13.0 21.5 %copy-start = (bf16[1,8,16,3072]{3,2,1,0:T(8,128)(2,1)S(1)}, bf16[1,8,16,3072]{3,2,1,0:T(8,128)(2,1)}, u32[]{:S(2)}) copy-start(bf16[1,8,16,3072]{3,2,1,0:T(8,128)(2,1)} %param.5) | copy-start | bytes 2359300
  16.3 18.2 %collective-permute-start = (bf16[2,48,3072]{2,1,0:T(8,128)(2,1)}, bf16[2,48,3072]{2,1,0:T(8,128)(2,1)}, u32[]{:S(2)}, u32[]{:S(2)}) collective-permute-start(bf16[2,48,3072]{2,1,0:T(8,128)(2,1)} %get-tuple-element.20), channel_id=1, source_target_pairs={{0,1},{1,2},{2,3},{3,4},{4,5},{5,6},{6,7},{7,8},{8,9},{9,10},{10,1... | collective-permute-start | bytes 1769480 | tf_op jit(solution)/shard_map/ppermute | solution.py:374
  18.2 16.3 %collective-permute-start.1 = (bf16[2,48,3072]{2,1,0:T(8,128)(2,1)}, bf16[2,48,3072]{2,1,0:T(8,128)(2,1)}, u32[]{:S(2)}, u32[]{:S(2)}) collective-permute-start(bf16[2,48,3072]{2,1,0:T(8,128)(2,1)} %get-tuple-element.21), channel_id=1, source_target_pairs={{1,0},{2,1},{3,2},{4,3},{5,4},{6,5},{7,6},{8,7},{9,8},{10,9},{11,1... | collective-permute-start | bytes 1769480 | tf_op jit(solution)/shard_map/ppermute | solution.py:375
  34.5 1.1 copy-start.1
  35.6 1.1 copy-start.3
  118.2 5.0 %copy-start.2 = (bf16[1,8,16,3072]{3,2,1,0:T(8,128)(2,1)S(1)}, bf16[1,8,16,3072]{3,2,1,0:T(8,128)(2,1)}, u32[]{:S(2)}) copy-start(bf16[1,8,16,3072]{3,2,1,0:T(8,128)(2,1)} %param.6) | copy-start | bytes 2359300
  118.2 5.0 %copy-start.4 = (bf16[1,8,16,3072]{3,2,1,0:T(8,128)(2,1)S(1)}, bf16[1,8,16,3072]{3,2,1,0:T(8,128)(2,1)}, u32[]{:S(2)}) copy-start(bf16[1,8,16,3072]{3,2,1,0:T(8,128)(2,1)} %param.4) | copy-start | bytes 2359300
  118.2 60.1 %all-to-all-start.2 = ((bf16[16,8,9216]{2,1,0:T(8,128)(2,1)}), bf16[16,8,9216]{2,1,0:T(8,128)(2,1)}, u32[]{:S(2)}, u32[]{:S(2)}) async-start(bf16[16,8,9216]{2,1,0:T(8,128)(2,1)} %shard_map.79), calls=%async_computation.2 | async-start | bytes 4718592 | tf_op jit(solution)/shard_map/all_to_all | solution.py:332
  130.3 15.3 %collective-permute-start.2 = (bf16[2,48,3072]{2,1,0:T(8,128)(2,1)S(1)}, bf16[2,48,3072]{2,1,0:T(8,128)(2,1)S(1)}, u32[]{:S(2)}, u32[]{:S(2)}) collective-permute-start(bf16[2,48,3072]{2,1,0:T(8,128)(2,1)S(1)} %get-tuple-element.29), channel_id=1, source_target_pairs={{0,1},{1,2},{2,3},{3,4},{4,5},{5,6},{6,7},{7,8},{8,9},{9,10},{10,1... | collective-permute-start | bytes 1769480 | tf_op jit(solution)/shard_map/ppermute | solution.py:445
  132.2 15.0 %collective-permute-start.3 = (bf16[2,48,3072]{2,1,0:T(8,128)(2,1)S(1)}, bf16[2,48,3072]{2,1,0:T(8,128)(2,1)S(1)}, u32[]{:S(2)}, u32[]{:S(2)}) collective-permute-start(bf16[2,48,3072]{2,1,0:T(8,128)(2,1)S(1)} %get-tuple-element.30), channel_id=1, source_target_pairs={{1,0},{2,1},{3,2},{4,3},{5,4},{6,5},{7,6},{8,7},{9,8},{10,9},{11,1... | collective-permute-start | bytes 1769480 | tf_op jit(solution)/shard_map/ppermute | solution.py:444

commit v3 on v2

--- a/solution.py
+++ b/solution.py
@@ -178,18 +178,14 @@
         store.wait()
 
 
-def temporal_grads_kernel(moved_ref, both_ref, probs_ref, out_ref, spatial_held, held, load_sems, store_sems):
+def temporal_grads_kernel(moved_ref, both_ref, probs_ref, out_ref, grad_ref, held, sems):
     frames = moved_ref.shape[0]
     width = TIME_HEADS * HEAD_DIM
     groups = range(HEADS // TIME_HEADS)
-    loads, stores = [], []
-    for group in groups:
-        at = slice(group * width, (group + 1) * width)
-        loads.append(started(both_ref.at[:, :, at], spatial_held.at[:, :, at], load_sems.at[group]))
+    stores = [started(both_ref.at[:, :, HEADS * HEAD_DIM :], grad_ref, sems.at[3 * len(groups)])]
     for group in groups:
         heads = range(group * TIME_HEADS, (group + 1) * TIME_HEADS)
-        loads[group].wait()
-        spatial = [head_rows(spatial_held, head) for head in heads]
+        spatial = [head_rows(both_ref, head) for head in heads]
         prob_grads = [
             dot(part, head_rows(moved_ref, 2 * HEADS + head), NT) for part, head in zip(spatial, heads)
         ]
@@ -208,11 +204,12 @@
             dot(part, head_rows(moved_ref, head), NN) * SCALING for part, head in zip(score_grads, heads)
         ]
         for place, parts in enumerate((outs, query_parts, key_parts)):
+            piece = group * 3 + place
             for step, part in enumerate(parts):
-                first = (group * 3 + place) * width + step * HEAD_DIM
+                first = piece * width + step * HEAD_DIM
                 held[:, :, first : first + HEAD_DIM] = chunked(part, frames).astype(BF16)
-        at = slice(group * 3 * width, (group + 1) * 3 * width)
-        stores.append(started(held.at[:, :, at], out_ref.at[:, :, at], store_sems.at[group]))
+            at = slice(piece * width, (piece + 1) * width)
+            stores.append(started(held.at[:, :, at], out_ref.at[:, :, at], sems.at[piece]))
     for store in stores:
         store.wait()
 
@@ -413,22 +410,16 @@
         input_output_aliases={1: 0},
         compiler_params=params,
     )(moved, in_hbm(sent))
-    both = in_hbm(exchange(sent))
-
-    parts_out = pl.pallas_call(
+    both = in_vmem(exchange(sent))
+
+    parts_out, spatial_grad = pl.pallas_call(
         temporal_grads_kernel,
-        in_specs=[in_place, anywhere, in_place],
-        out_specs=anywhere,
-        out_shape=pltpu.HBM(joined_shape, BF16),
-        scratch_shapes=[
-            pltpu.VMEM((parts, spots, channels), BF16),
-            pltpu.VMEM(joined_shape, BF16),
-            pltpu.SemaphoreType.DMA((groups,)),
-            pltpu.SemaphoreType.DMA((groups,)),
-        ],
+        in_specs=[in_place] * 3,
+        out_specs=[anywhere] * 2,
+        out_shape=[pltpu.HBM(joined_shape, BF16), pltpu.HBM((parts, spots, channels), BF16)],
+        scratch_shapes=[pltpu.VMEM(joined_shape, BF16), pltpu.SemaphoreType.DMA((3 * groups + 1,))],
         compiler_params=params,
     )(moved, both, in_vmem(probs))
-    parts_out, both = lax.optimization_barrier((parts_out, both))
     back = exchange(parts_out)
 
     count = HEADS // BWD_HEADS
@@ -437,10 +428,10 @@
     qs, ks, vs, to_low, to_high = call(
         functools.partial(spatial_bwd_kernel, total_rows, breadth),
         count,
-        [scalar, own, own, own, rims_block(BWD_HEADS), rims_block(BWD_HEADS), chunk_block(BWD_HEADS, count)],
+        [scalar, own, own, own, rims_block(BWD_HEADS), rims_block(BWD_HEADS), chunk_block(BWD_HEADS, 0)],
         [chunk_block(BWD_HEADS, 0), own, own, rims_block(BWD_HEADS), rims_block(BWD_HEADS)],
         [pltpu.HBM((parts, spots, channels), BF16), whole, whole, rims, rims],
-    )(first_row, query, key, value, low, high, in_hbm(both))
+    )(first_row, query, key, value, low, high, in_hbm(spatial_grad))
     from_high = lax.ppermute(to_low, "rows", downward)
     from_low = lax.ppermute(to_high, "rows", upward)
     final = jax.ShapeDtypeStruct((tokens, channels), BF16)

time: 182 us -> 181 us (level)
  no operation moved by 1% of the time
where the time goes in v3:
time: 181 us; the launch traced here: 180 us
  waiting for transfers between devices  73.7 us (41%)
  blocking collectives  44.2 us (24%)
  starting transfers between devices  30.5 us (17%)
  Pallas kernels  28.8 us (16%)
  local copies, waits for them, and re-layouts  2.28 us (1%)
    all_to_all x2, waiting for transfers between devices, exchange(): return lax.all_to_all(chunks, 'tm', split_axis=0, concat_axis=0, tiled=True)  54.6 us
    all_to_all x1, blocking collectives, exchange(): return lax.all_to_all(chunks, 'tm', split_axis=0, concat_axis=0, tiled=True)  44.2 us
    all_to_all x2, starting transfers between devices, exchange(): return lax.all_to_all(chunks, 'tm', split_axis=0, concat_axis=0, tiled=True)  14.6 us
    ppermute x1, waiting for transfers between devices, on_device(): low = lax.ppermute(to_high, 'rows', upward)  10.2 us
    ppermute x1, waiting for transfers between devices, on_device(): from_low = lax.ppermute(to_high, 'rows', upward)  7.38 us
    pallas_call x1, Pallas kernels, on_device(): call(functools.partial(spatial_bwd_kernel, total_rows, breadth), count, [...  6.98 us
    pallas_call x1, Pallas kernels, on_device(): call(functools.partial(spatial_fwd_kernel, total_rows, breadth), HEADS //...  6.16 us
    ppermute x1, starting transfers between devices, on_device(): high = lax.ppermute(to_low, 'rows', downward)  6.05 us
  transfers between devices with their start and end apart: 6, of which 5 were waited for; matrix products, arithmetic and copies ran while one was open for 0% of the time, Pallas kernels for 10%

profile of v3, /device:TPU:6, one launch (start us, length us, event | category | flops | bytes accessed | tf_op | source)
XLA Modules:
  0.0 180.3 jit_solution(997345259515346981)
XLA Ops:
  0.6 2.7 %shard_map.75 = bf16[16,8,9216]{2,1,0:T(8,128)(2,1)} custom-call(bf16[16,8,3072]{2,1,0:T(8,128)(2,1)} %bitcast.20, bf16[16,8,3072]{2,1,0:T(8,128)(2,1)} %bitcast.11, bf16[16,8,3072]{2,1,0:T(8,128)(2,1)} %bitcast.23), custom_call_target="tpu_custom_call" | custom-call | tf_op jit(solution)/shard_map/pallas_call | solution.py:375
  3.4 9.6 %all-to-all-start = ((bf16[16,8,9216]{2,1,0:T(8,128)(2,1)}), bf16[16,8,9216]{2,1,0:T(8,128)(2,1)S(1)}, u32[]{:S(2)}, u32[]{:S(2)}) async-start(bf16[16,8,9216]{2,1,0:T(8,128)(2,1)} %shard_map.75), calls=%async_computation | async-start | bytes 4718592 | tf_op jit(solution)/shard_map/all_to_all | solution.py:329
  13.0 0.0 copy-start
  13.0 3.3 %shard_map.76 = (bf16[2,48,3072]{2,1,0:T(8,128)(2,1)}, bf16[2,48,3072]{2,1,0:T(8,128)(2,1)}) custom-call(bf16[128,3072]{1,0:T(8,128)(2,1)} %bitcast.12, bf16[128,3072]{1,0:T(8,128)(2,1)} %bitcast.16, bf16[128,3072]{1,0:T(8,128)(2,1)} %bitcast.13, bf16[128,3072]{1,0:T(8,128)(2,1)} %bitcast.17), custom_call_target="tpu_custom_call" | custom-call | tf_op jit(solution)/shard_map/pallas_call | solution.py:364
  16.3 1.9 %collective-permute-start = (bf16[2,48,3072]{2,1,0:T(8,128)(2,1)}, bf16[2,48,3072]{2,1,0:T(8,128)(2,1)}, u32[]{:S(2)}, u32[]{:S(2)}) collective-permute-start(bf16[2,48,3072]{2,1,0:T(8,128)(2,1)} %get-tuple-element.20), channel_id=1, source_target_pairs={{0,1},{1,2},{2,3},{3,4},{4,5},{5,6},{6,7},{7,8},{8,9},{9,10},{10,1... | collective-permute-start | bytes 1769480 | tf_op jit(solution)/shard_map/ppermute | solution.py:371
  18.2 6.0 %collective-permute-start.1 = (bf16[2,48,3072]{2,1,0:T(8,128)(2,1)}, bf16[2,48,3072]{2,1,0:T(8,128)(2,1)}, u32[]{:S(2)}, u32[]{:S(2)}) collective-permute-start(bf16[2,48,3072]{2,1,0:T(8,128)(2,1)} %get-tuple-element.21), channel_id=1, source_target_pairs={{1,0},{2,1},{3,2},{4,3},{5,4},{6,5},{7,6},{8,7},{9,8},{10,9},{11,1... | collective-permute-start | bytes 1769480 | tf_op jit(solution)/shard_map/ppermute | solution.py:372
  24.2 10.2 %collective-permute-done.low_ref = bf16[2,48,3072]{2,1,0:T(8,128)(2,1)} collective-permute-done((bf16[2,48,3072]{2,1,0:T(8,128)(2,1)}, bf16[2,48,3072]{2,1,0:T(8,128)(2,1)}, u32[]{:S(2)}, u32[]{:S(2)}) %collective-permute-start) | collective-permute-done | bytes 589856 | tf_op jit(solution)/shard_map/ppermute | solution.py:371
  34.5 0.0 collective-permute-done.1.high_ref
  34.5 0.0 copy-done
  34.5 0.0 copy-start.1
  34.5 1.1 copy-done.1
  35.6 0.0 copy-start.3
  35.6 1.1 copy-done.3
  36.7 6.2 %shard_map.77.begun_ref = bf16[16,8,6144]{2,1,0:T(8,128)(2,1)} custom-call(s32[1]{0:T(128)} %bitcast.3.first_ref, bf16[128,3072]{1,0:T(8,128)(2,1)S(1)} %bitcast.21, bf16[128,3072]{1,0:T(8,128)(2,1)S(1)} %bitcast.14, bf16[128,3072]{1,0:T(8,128)(2,1)S(1)} %bitcast.18, bf16[2,48,3072]{2,1,0:T(8,128)(2,1)} %collective-permute-done.low_ref, ...), custom_call_target="tpu_custom_call" | custom-call | tf_op jit(solution)/shard_map/pallas_call | solution.py:390
  42.9 25.0 %all-to-all-done.moved_ref = bf16[16,8,9216]{2,1,0:T(8,128)(2,1)S(1)} async-done(((bf16[16,8,9216]{2,1,0:T(8,128)(2,1)}), bf16[16,8,9216]{2,1,0:T(8,128)(2,1)S(1)}, u32[]{:S(2)}, u32[]{:S(2)}) %all-to-all-start) | async-done | bytes 2359328 | tf_op jit(solution)/shard_map/all_to_all | solution.py:329
  67.9 2.1 %shard_map.78 = (bf16[16,8,6144]{2,1,0:T(8,128)(2,1)}, f32[24,128,128]{2,1,0:T(8,128)S(1)}) custom-call(bf16[16,8,9216]{2,1,0:T(8,128)(2,1)S(1)} %all-to-all-done.moved_ref, bf16[16,8,6144]{2,1,0:T(8,128)(2,1)} %shard_map.77.begun_ref), custom_call_target="tpu_custom_call", output_to_operand_aliasing={{0}: (1, {})} | custom-call | tf_op jit(solution)/shard_map/pallas_call | solution.py:401
  70.1 44.2 %all_to_all.15.both_ref = bf16[16,8,6144]{2,1,0:T(8,128)(2,1)S(1)} all-to-all(bf16[16,8,6144]{2,1,0:T(8,128)(2,1)} %get-tuple-element.22), channel_id=1, replica_groups=mesh['tm'=16,'rows'=16] {'tm'}, dimensions={0} | all-to-all | bytes 3145728 | tf_op jit(solution)/shard_map/all_to_all | solution.py:329
  114.3 2.5 %shard_map.79 = (bf16[16,8,9216]{2,1,0:T(8,128)(2,1)}, bf16[16,8,3072]{2,1,0:T(8,128)(2,1)}) custom-call(bf16[16,8,9216]{2,1,0:T(8,128)(2,1)S(1)} %all-to-all-done.moved_ref, bf16[16,8,6144]{2,1,0:T(8,128)(2,1)S(1)} %all_to_all.15.both_ref, f32[24,128,128]{2,1,0:T(8,128)S(1)} %get-tuple-element.23.probs_ref), custom_call_target="tpu_custom_call" | custom-call | tf_op jit(solution)/shard_map/pallas_call | solution.py:415
  116.8 0.0 copy-start.2
  116.8 0.0 copy-start.4
  116.8 5.0 %all-to-all-start.2 = ((bf16[16,8,9216]{2,1,0:T(8,128)(2,1)}), bf16[16,8,9216]{2,1,0:T(8,128)(2,1)}, u32[]{:S(2)}, u32[]{:S(2)}) async-start(bf16[16,8,9216]{2,1,0:T(8,128)(2,1)} %get-tuple-element.24), calls=%async_computation.2 | async-start | bytes 4718592 | tf_op jit(solution)/shard_map/all_to_all | solution.py:329
  121.8 0.0 copy-done.2
  121.8 0.0 copy-done.4
  121.8 7.0 %shard_map.80 = (bf16[16,8,3072]{2,1,0:T(8,128)(2,1)}, f32[128,3072]{1,0:T(8,128)S(1)}, f32[128,3072]{1,0:T(8,128)S(1)}, bf16[2,48,3072]{2,1,0:T(8,128)(2,1)S(1)}, bf16[2,48,3072]{2,1,0:T(8,128)(2,1)S(1)}) custom-call(s32[1]{0:T(128)} %bitcast.3.first_ref, bf16[128,3072]{1,0:T(8,128)(2,1)S(1)} %bitcast.22, bf16[128,3072]{1,0:T(8,128)(2,1)S(1)} %bitcast.15, ...), custom_call_target="tpu_custom_call" | custom-call | tf_op jit(solution)/shard_map/pallas_call | solution.py:428
  128.8 1.9 %collective-permute-start.2 = (bf16[2,48,3072]{2,1,0:T(8,128)(2,1)S(1)}, bf16[2,48,3072]{2,1,0:T(8,128)(2,1)S(1)}, u32[]{:S(2)}, u32[]{:S(2)}) collective-permute-start(bf16[2,48,3072]{2,1,0:T(8,128)(2,1)S(1)} %get-tuple-element.29), channel_id=1, source_target_pairs={{0,1},{1,2},{2,3},{3,4},{4,5},{5,6},{6,7},{7,8},{8,9},{9,10},{10,1... | collective-permute-start | bytes 1769480 | tf_op jit(solution)/shard_map/ppermute | solution.py:436
  130.7 6.0 %collective-permute-start.3 = (bf16[2,48,3072]{2,1,0:T(8,128)(2,1)S(1)}, bf16[2,48,3072]{2,1,0:T(8,128)(2,1)S(1)}, u32[]{:S(2)}, u32[]{:S(2)}) collective-permute-start(bf16[2,48,3072]{2,1,0:T(8,128)(2,1)S(1)} %get-tuple-element.30), channel_id=1, source_target_pairs={{1,0},{2,1},{3,2},{4,3},{5,4},{6,5},{7,6},{8,7},{9,8},{10,9},{11,1... | collective-permute-start | bytes 1769480 | tf_op jit(solution)/shard_map/ppermute | solution.py:435
  136.8 7.4 %collective-permute-done.2.from_low_ref = bf16[2,48,3072]{2,1,0:T(8,128)(2,1)S(1)} collective-permute-done((bf16[2,48,3072]{2,1,0:T(8,128)(2,1)S(1)}, bf16[2,48,3072]{2,1,0:T(8,128)(2,1)S(1)}, u32[]{:S(2)}, u32[]{:S(2)}) %collective-permute-start.2) | collective-permute-done | bytes 589856 | tf_op jit(solution)/shard_map/ppermute | solution.py:436
  144.2 1.5 collective-permute-done.3.from_high_ref
  145.7 1.9 %shard_map.81 = (bf16[16,8,3072]{2,1,0:T(8,128)(2,1)}, bf16[128,3072]{1,0:T(8,128)(2,1)}) custom-call(f32[128,3072]{1,0:T(8,128)S(1)} %get-tuple-element.27.ks_ref, f32[128,3072]{1,0:T(8,128)S(1)} %get-tuple-element.28.vs_ref, bf16[2,48,3072]{2,1,0:T(8,128)(2,1)S(1)} %collective-permute-done.2.from_low_ref, ...), custom_call_target="tpu_custom_call" | custom-call | tf_op jit(solution)/shard_map/pallas_call | solution.py:439
  147.6 29.5 %all-to-all-done.2.back_ref = bf16[16,8,9216]{2,1,0:T(8,128)(2,1)} async-done(((bf16[16,8,9216]{2,1,0:T(8,128)(2,1)}), bf16[16,8,9216]{2,1,0:T(8,128)(2,1)}, u32[]{:S(2)}, u32[]{:S(2)}) %all-to-all-start.2) | async-done | bytes 2359328 | tf_op jit(solution)/shard_map/all_to_all | solution.py:329
  177.2 3.1 %shard_map.82 = (bf16[16,8,3072]{2,1,0:T(8,128)(2,1)}, bf16[16,8,3072]{2,1,0:T(8,128)(2,1)}, bf16[16,8,3072]{2,1,0:T(8,128)(2,1)}) custom-call(bf16[16,8,9216]{2,1,0:T(8,128)(2,1)} %all-to-all-done.2.back_ref, bf16[16,8,3072]{2,1,0:T(8,128)(2,1)} %get-tuple-element.26.qs_ref, bf16[16,8,3072]{2,1,0:T(8,128)(2,1)} %get-tuple-element.31.ks_ref), custom_call_target="tpu_custom_call" | custom-call | tf_op jit(solution)/shard_map/pallas_call | solution.py:447
Async XLA Ops:
  3.4 64.6 %all-to-all-start = ((bf16[16,8,9216]{2,1,0:T(8,128)(2,1)}), bf16[16,8,9216]{2,1,0:T(8,128)(2,1)S(1)}, u32[]{:S(2)}, u32[]{:S(2)}) async-start(bf16[16,8,9216]{2,1,0:T(8,128)(2,1)} %shard_map.75), calls=%async_computation | async-start | bytes 4718592 | tf_op jit(solution)/shard_map/all_to_all | solution.py:329
  13.0 21.5 %copy-start = (bf16[1,8,16,3072]{3,2,1,0:T(8,128)(2,1)S(1)}, bf16[1,8,16,3072]{3,2,1,0:T(8,128)(2,1)}, u32[]{:S(2)}) copy-start(bf16[1,8,16,3072]{3,2,1,0:T(8,128)(2,1)} %param.5) | copy-start | bytes 2359300
  16.3 18.2 %collective-permute-start = (bf16[2,48,3072]{2,1,0:T(8,128)(2,1)}, bf16[2,48,3072]{2,1,0:T(8,128)(2,1)}, u32[]{:S(2)}, u32[]{:S(2)}) collective-permute-start(bf16[2,48,3072]{2,1,0:T(8,128)(2,1)} %get-tuple-element.20), channel_id=1, source_target_pairs={{0,1},{1,2},{2,3},{3,4},{4,5},{5,6},{6,7},{7,8},{8,9},{9,10},{10,1... | collective-permute-start | bytes 1769480 | tf_op jit(solution)/shard_map/ppermute | solution.py:371
  18.2 16.3 %collective-permute-start.1 = (bf16[2,48,3072]{2,1,0:T(8,128)(2,1)}, bf16[2,48,3072]{2,1,0:T(8,128)(2,1)}, u32[]{:S(2)}, u32[]{:S(2)}) collective-permute-start(bf16[2,48,3072]{2,1,0:T(8,128)(2,1)} %get-tuple-element.21), channel_id=1, source_target_pairs={{1,0},{2,1},{3,2},{4,3},{5,4},{6,5},{7,6},{8,7},{9,8},{10,9},{11,1... | collective-permute-start | bytes 1769480 | tf_op jit(solution)/shard_map/ppermute | solution.py:372
  34.5 1.1 copy-start.1
  35.6 1.1 copy-start.3
  116.8 5.0 %copy-start.2 = (bf16[1,8,16,3072]{3,2,1,0:T(8,128)(2,1)S(1)}, bf16[1,8,16,3072]{3,2,1,0:T(8,128)(2,1)}, u32[]{:S(2)}) copy-start(bf16[1,8,16,3072]{3,2,1,0:T(8,128)(2,1)} %param.6) | copy-start | bytes 2359300
  116.8 5.0 %copy-start.4 = (bf16[1,8,16,3072]{3,2,1,0:T(8,128)(2,1)S(1)}, bf16[1,8,16,3072]{3,2,1,0:T(8,128)(2,1)}, u32[]{:S(2)}) copy-start(bf16[1,8,16,3072]{3,2,1,0:T(8,128)(2,1)} %param.4) | copy-start | bytes 2359300
  116.8 60.4 %all-to-all-start.2 = ((bf16[16,8,9216]{2,1,0:T(8,128)(2,1)}), bf16[16,8,9216]{2,1,0:T(8,128)(2,1)}, u32[]{:S(2)}, u32[]{:S(2)}) async-start(bf16[16,8,9216]{2,1,0:T(8,128)(2,1)} %get-tuple-element.24), calls=%async_computation.2 | async-start | bytes 4718592 | tf_op jit(solution)/shard_map/all_to_all | solution.py:329
  128.8 15.4 %collective-permute-start.2 = (bf16[2,48,3072]{2,1,0:T(8,128)(2,1)S(1)}, bf16[2,48,3072]{2,1,0:T(8,128)(2,1)S(1)}, u32[]{:S(2)}, u32[]{:S(2)}) collective-permute-start(bf16[2,48,3072]{2,1,0:T(8,128)(2,1)S(1)} %get-tuple-element.29), channel_id=1, source_target_pairs={{0,1},{1,2},{2,3},{3,4},{4,5},{5,6},{6,7},{7,8},{8,9},{9,10},{10,1... | collective-permute-start | bytes 1769480 | tf_op jit(solution)/shard_map/ppermute | solution.py:436
  130.7 15.0 %collective-permute-start.3 = (bf16[2,48,3072]{2,1,0:T(8,128)(2,1)S(1)}, bf16[2,48,3072]{2,1,0:T(8,128)(2,1)S(1)}, u32[]{:S(2)}, u32[]{:S(2)}) collective-permute-start(bf16[2,48,3072]{2,1,0:T(8,128)(2,1)S(1)} %get-tuple-element.30), channel_id=1, source_target_pairs={{1,0},{2,1},{3,2},{4,3},{5,4},{6,5},{7,6},{8,7},{9,8},{10,9},{11,1... | collective-permute-start | bytes 1769480 | tf_op jit(solution)/shard_map/ppermute | solution.py:435

commit v4 on v3

--- a/solution.py
+++ b/solution.py
@@ -16,7 +16,7 @@
 F32 = jnp.float32
 
 FWD_HEADS = 4
-TIME_HEADS = 8
+TIME_HEADS = 12
 BWD_HEADS = 4
 RIM_HEADS = 8
 PIECES = 4

time: 181 us -> 181 us (level)
  no operation moved by 1% of the time
where the time goes in v4:
time: 181 us; the launch traced here: 180 us
  waiting for transfers between devices  73.7 us (41%)
  blocking collectives  44.2 us (24%)
  starting transfers between devices  30.5 us (17%)
  Pallas kernels  28.5 us (16%)
  local copies, waits for them, and re-layouts  2.28 us (1%)
    all_to_all x2, waiting for transfers between devices, exchange(): return lax.all_to_all(chunks, 'tm', split_axis=0, concat_axis=0, tiled=True)  54.6 us
    all_to_all x1, blocking collectives, exchange(): return lax.all_to_all(chunks, 'tm', split_axis=0, concat_axis=0, tiled=True)  44.2 us
    all_to_all x2, starting transfers between devices, exchange(): return lax.all_to_all(chunks, 'tm', split_axis=0, concat_axis=0, tiled=True)  14.6 us
    ppermute x1, waiting for transfers between devices, on_device(): low = lax.ppermute(to_high, 'rows', upward)  10.2 us
    ppermute x1, waiting for transfers between devices, on_device(): from_low = lax.ppermute(to_high, 'rows', upward)  7.38 us
    pallas_call x1, Pallas kernels, on_device(): call(functools.partial(spatial_bwd_kernel, total_rows, breadth), count, [...  6.98 us
    pallas_call x1, Pallas kernels, on_device(): call(functools.partial(spatial_fwd_kernel, total_rows, breadth), HEADS //...  6.16 us
    ppermute x1, starting transfers between devices, on_device(): high = lax.ppermute(to_low, 'rows', downward)  6.05 us
  transfers between devices with their start and end apart: 6, of which 5 were waited for; matrix products, arithmetic and copies ran while one was open for 0% of the time, Pallas kernels for 10%

profile of v4, /device:TPU:6, one launch (start us, length us, event | category | flops | bytes accessed | tf_op | source)
XLA Modules:
  0.0 180.0 jit_solution(10725745696818236475)
XLA Ops:
  0.6 2.7 %shard_map.75 = bf16[16,8,9216]{2,1,0:T(8,128)(2,1)} custom-call(bf16[16,8,3072]{2,1,0:T(8,128)(2,1)} %bitcast.20, bf16[16,8,3072]{2,1,0:T(8,128)(2,1)} %bitcast.11, bf16[16,8,3072]{2,1,0:T(8,128)(2,1)} %bitcast.23), custom_call_target="tpu_custom_call" | custom-call | tf_op jit(solution)/shard_map/pallas_call | solution.py:375
  3.4 9.6 %all-to-all-start = ((bf16[16,8,9216]{2,1,0:T(8,128)(2,1)}), bf16[16,8,9216]{2,1,0:T(8,128)(2,1)S(1)}, u32[]{:S(2)}, u32[]{:S(2)}) async-start(bf16[16,8,9216]{2,1,0:T(8,128)(2,1)} %shard_map.75), calls=%async_computation | async-start | bytes 4718592 | tf_op jit(solution)/shard_map/all_to_all | solution.py:329
  13.0 0.0 copy-start
  13.0 3.3 %shard_map.76 = (bf16[2,48,3072]{2,1,0:T(8,128)(2,1)}, bf16[2,48,3072]{2,1,0:T(8,128)(2,1)}) custom-call(bf16[128,3072]{1,0:T(8,128)(2,1)} %bitcast.12, bf16[128,3072]{1,0:T(8,128)(2,1)} %bitcast.16, bf16[128,3072]{1,0:T(8,128)(2,1)} %bitcast.13, bf16[128,3072]{1,0:T(8,128)(2,1)} %bitcast.17), custom_call_target="tpu_custom_call" | custom-call | tf_op jit(solution)/shard_map/pallas_call | solution.py:364
  16.3 1.9 %collective-permute-start = (bf16[2,48,3072]{2,1,0:T(8,128)(2,1)}, bf16[2,48,3072]{2,1,0:T(8,128)(2,1)}, u32[]{:S(2)}, u32[]{:S(2)}) collective-permute-start(bf16[2,48,3072]{2,1,0:T(8,128)(2,1)} %get-tuple-element.20), channel_id=1, source_target_pairs={{0,1},{1,2},{2,3},{3,4},{4,5},{5,6},{6,7},{7,8},{8,9},{9,10},{10,1... | collective-permute-start | bytes 1769480 | tf_op jit(solution)/shard_map/ppermute | solution.py:371
  18.2 6.0 %collective-permute-start.1 = (bf16[2,48,3072]{2,1,0:T(8,128)(2,1)}, bf16[2,48,3072]{2,1,0:T(8,128)(2,1)}, u32[]{:S(2)}, u32[]{:S(2)}) collective-permute-start(bf16[2,48,3072]{2,1,0:T(8,128)(2,1)} %get-tuple-element.21), channel_id=1, source_target_pairs={{1,0},{2,1},{3,2},{4,3},{5,4},{6,5},{7,6},{8,7},{9,8},{10,9},{11,1... | collective-permute-start | bytes 1769480 | tf_op jit(solution)/shard_map/ppermute | solution.py:372
  24.2 10.2 %collective-permute-done.low_ref = bf16[2,48,3072]{2,1,0:T(8,128)(2,1)} collective-permute-done((bf16[2,48,3072]{2,1,0:T(8,128)(2,1)}, bf16[2,48,3072]{2,1,0:T(8,128)(2,1)}, u32[]{:S(2)}, u32[]{:S(2)}) %collective-permute-start) | collective-permute-done | bytes 589856 | tf_op jit(solution)/shard_map/ppermute | solution.py:371
  34.5 0.0 collective-permute-done.1.high_ref
  34.5 0.0 copy-done
  34.5 0.0 copy-start.1
  34.5 1.1 copy-done.1
  35.6 0.0 copy-start.3
  35.6 1.1 copy-done.3
  36.7 6.2 %shard_map.77.begun_ref = bf16[16,8,6144]{2,1,0:T(8,128)(2,1)} custom-call(s32[1]{0:T(128)} %bitcast.3.first_ref, bf16[128,3072]{1,0:T(8,128)(2,1)S(1)} %bitcast.21, bf16[128,3072]{1,0:T(8,128)(2,1)S(1)} %bitcast.14, bf16[128,3072]{1,0:T(8,128)(2,1)S(1)} %bitcast.18, bf16[2,48,3072]{2,1,0:T(8,128)(2,1)} %collective-permute-done.low_ref, ...), custom_call_target="tpu_custom_call" | custom-call | tf_op jit(solution)/shard_map/pallas_call | solution.py:390
  42.9 25.0 %all-to-all-done.moved_ref = bf16[16,8,9216]{2,1,0:T(8,128)(2,1)S(1)} async-done(((bf16[16,8,9216]{2,1,0:T(8,128)(2,1)}), bf16[16,8,9216]{2,1,0:T(8,128)(2,1)S(1)}, u32[]{:S(2)}, u32[]{:S(2)}) %all-to-all-start) | async-done | bytes 2359328 | tf_op jit(solution)/shard_map/all_to_all | solution.py:329
  67.9 2.1 %shard_map.78 = (bf16[16,8,6144]{2,1,0:T(8,128)(2,1)}, f32[24,128,128]{2,1,0:T(8,128)S(1)}) custom-call(bf16[16,8,9216]{2,1,0:T(8,128)(2,1)S(1)} %all-to-all-done.moved_ref, bf16[16,8,6144]{2,1,0:T(8,128)(2,1)} %shard_map.77.begun_ref), custom_call_target="tpu_custom_call", output_to_operand_aliasing={{0}: (1, {})} | custom-call | tf_op jit(solution)/shard_map/pallas_call | solution.py:401
  70.0 44.2 %all_to_all.15.both_ref = bf16[16,8,6144]{2,1,0:T(8,128)(2,1)S(1)} all-to-all(bf16[16,8,6144]{2,1,0:T(8,128)(2,1)} %get-tuple-element.22), channel_id=1, replica_groups=mesh['tm'=16,'rows'=16] {'tm'}, dimensions={0} | all-to-all | bytes 3145728 | tf_op jit(solution)/shard_map/all_to_all | solution.py:329
  114.2 2.3 %shard_map.79 = (bf16[16,8,9216]{2,1,0:T(8,128)(2,1)}, bf16[16,8,3072]{2,1,0:T(8,128)(2,1)}) custom-call(bf16[16,8,9216]{2,1,0:T(8,128)(2,1)S(1)} %all-to-all-done.moved_ref, bf16[16,8,6144]{2,1,0:T(8,128)(2,1)S(1)} %all_to_all.15.both_ref, f32[24,128,128]{2,1,0:T(8,128)S(1)} %get-tuple-element.23.probs_ref), custom_call_target="tpu_custom_call" | custom-call | tf_op jit(solution)/shard_map/pallas_call | solution.py:415
  116.5 0.0 copy-start.2
  116.5 0.0 copy-start.4
  116.5 5.0 %all-to-all-start.2 = ((bf16[16,8,9216]{2,1,0:T(8,128)(2,1)}), bf16[16,8,9216]{2,1,0:T(8,128)(2,1)}, u32[]{:S(2)}, u32[]{:S(2)}) async-start(bf16[16,8,9216]{2,1,0:T(8,128)(2,1)} %get-tuple-element.24), calls=%async_computation.2 | async-start | bytes 4718592 | tf_op jit(solution)/shard_map/all_to_all | solution.py:329
  121.5 0.0 copy-done.2
  121.5 0.0 copy-done.4
  121.6 7.0 %shard_map.80 = (bf16[16,8,3072]{2,1,0:T(8,128)(2,1)}, f32[128,3072]{1,0:T(8,128)S(1)}, f32[128,3072]{1,0:T(8,128)S(1)}, bf16[2,48,3072]{2,1,0:T(8,128)(2,1)S(1)}, bf16[2,48,3072]{2,1,0:T(8,128)(2,1)S(1)}) custom-call(s32[1]{0:T(128)} %bitcast.3.first_ref, bf16[128,3072]{1,0:T(8,128)(2,1)S(1)} %bitcast.22, bf16[128,3072]{1,0:T(8,128)(2,1)S(1)} %bitcast.15, ...), custom_call_target="tpu_custom_call" | custom-call | tf_op jit(solution)/shard_map/pallas_call | solution.py:428
  128.5 1.9 %collective-permute-start.2 = (bf16[2,48,3072]{2,1,0:T(8,128)(2,1)S(1)}, bf16[2,48,3072]{2,1,0:T(8,128)(2,1)S(1)}, u32[]{:S(2)}, u32[]{:S(2)}) collective-permute-start(bf16[2,48,3072]{2,1,0:T(8,128)(2,1)S(1)} %get-tuple-element.29), channel_id=1, source_target_pairs={{0,1},{1,2},{2,3},{3,4},{4,5},{5,6},{6,7},{7,8},{8,9},{9,10},{10,1... | collective-permute-start | bytes 1769480 | tf_op jit(solution)/shard_map/ppermute | solution.py:436
  130.5 6.0 %collective-permute-start.3 = (bf16[2,48,3072]{2,1,0:T(8,128)(2,1)S(1)}, bf16[2,48,3072]{2,1,0:T(8,128)(2,1)S(1)}, u32[]{:S(2)}, u32[]{:S(2)}) collective-permute-start(bf16[2,48,3072]{2,1,0:T(8,128)(2,1)S(1)} %get-tuple-element.30), channel_id=1, source_target_pairs={{1,0},{2,1},{3,2},{4,3},{5,4},{6,5},{7,6},{8,7},{9,8},{10,9},{11,1... | collective-permute-start | bytes 1769480 | tf_op jit(solution)/shard_map/ppermute | solution.py:435
  136.5 7.4 %collective-permute-done.2.from_low_ref = bf16[2,48,3072]{2,1,0:T(8,128)(2,1)S(1)} collective-permute-done((bf16[2,48,3072]{2,1,0:T(8,128)(2,1)S(1)}, bf16[2,48,3072]{2,1,0:T(8,128)(2,1)S(1)}, u32[]{:S(2)}, u32[]{:S(2)}) %collective-permute-start.2) | collective-permute-done | bytes 589856 | tf_op jit(solution)/shard_map/ppermute | solution.py:436
  143.9 1.5 collective-permute-done.3.from_high_ref
  145.4 1.9 %shard_map.81 = (bf16[16,8,3072]{2,1,0:T(8,128)(2,1)}, bf16[128,3072]{1,0:T(8,128)(2,1)}) custom-call(f32[128,3072]{1,0:T(8,128)S(1)} %get-tuple-element.27.ks_ref, f32[128,3072]{1,0:T(8,128)S(1)} %get-tuple-element.28.vs_ref, bf16[2,48,3072]{2,1,0:T(8,128)(2,1)S(1)} %collective-permute-done.2.from_low_ref, ...), custom_call_target="tpu_custom_call" | custom-call | tf_op jit(solution)/shard_map/pallas_call | solution.py:439
  147.3 29.6 %all-to-all-done.2.back_ref = bf16[16,8,9216]{2,1,0:T(8,128)(2,1)} async-done(((bf16[16,8,9216]{2,1,0:T(8,128)(2,1)}), bf16[16,8,9216]{2,1,0:T(8,128)(2,1)}, u32[]{:S(2)}, u32[]{:S(2)}) %all-to-all-start.2) | async-done | bytes 2359328 | tf_op jit(solution)/shard_map/all_to_all | solution.py:329
  176.9 3.1 %shard_map.82 = (bf16[16,8,3072]{2,1,0:T(8,128)(2,1)}, bf16[16,8,3072]{2,1,0:T(8,128)(2,1)}, bf16[16,8,3072]{2,1,0:T(8,128)(2,1)}) custom-call(bf16[16,8,9216]{2,1,0:T(8,128)(2,1)} %all-to-all-done.2.back_ref, bf16[16,8,3072]{2,1,0:T(8,128)(2,1)} %get-tuple-element.26.qs_ref, bf16[16,8,3072]{2,1,0:T(8,128)(2,1)} %get-tuple-element.31.ks_ref), custom_call_target="tpu_custom_call" | custom-call | tf_op jit(solution)/shard_map/pallas_call | solution.py:447
Async XLA Ops:
  3.4 64.6 %all-to-all-start = ((bf16[16,8,9216]{2,1,0:T(8,128)(2,1)}), bf16[16,8,9216]{2,1,0:T(8,128)(2,1)S(1)}, u32[]{:S(2)}, u32[]{:S(2)}) async-start(bf16[16,8,9216]{2,1,0:T(8,128)(2,1)} %shard_map.75), calls=%async_computation | async-start | bytes 4718592 | tf_op jit(solution)/shard_map/all_to_all | solution.py:329
  13.0 21.5 %copy-start = (bf16[1,8,16,3072]{3,2,1,0:T(8,128)(2,1)S(1)}, bf16[1,8,16,3072]{3,2,1,0:T(8,128)(2,1)}, u32[]{:S(2)}) copy-start(bf16[1,8,16,3072]{3,2,1,0:T(8,128)(2,1)} %param.5) | copy-start | bytes 2359300
  16.3 18.2 %collective-permute-start = (bf16[2,48,3072]{2,1,0:T(8,128)(2,1)}, bf16[2,48,3072]{2,1,0:T(8,128)(2,1)}, u32[]{:S(2)}, u32[]{:S(2)}) collective-permute-start(bf16[2,48,3072]{2,1,0:T(8,128)(2,1)} %get-tuple-element.20), channel_id=1, source_target_pairs={{0,1},{1,2},{2,3},{3,4},{4,5},{5,6},{6,7},{7,8},{8,9},{9,10},{10,1... | collective-permute-start | bytes 1769480 | tf_op jit(solution)/shard_map/ppermute | solution.py:371
  18.2 16.3 %collective-permute-start.1 = (bf16[2,48,3072]{2,1,0:T(8,128)(2,1)}, bf16[2,48,3072]{2,1,0:T(8,128)(2,1)}, u32[]{:S(2)}, u32[]{:S(2)}) collective-permute-start(bf16[2,48,3072]{2,1,0:T(8,128)(2,1)} %get-tuple-element.21), channel_id=1, source_target_pairs={{1,0},{2,1},{3,2},{4,3},{5,4},{6,5},{7,6},{8,7},{9,8},{10,9},{11,1... | collective-permute-start | bytes 1769480 | tf_op jit(solution)/shard_map/ppermute | solution.py:372
  34.5 1.1 copy-start.1
  35.6 1.1 copy-start.3
  116.5 5.0 %copy-start.2 = (bf16[1,8,16,3072]{3,2,1,0:T(8,128)(2,1)S(1)}, bf16[1,8,16,3072]{3,2,1,0:T(8,128)(2,1)}, u32[]{:S(2)}) copy-start(bf16[1,8,16,3072]{3,2,1,0:T(8,128)(2,1)} %param.6) | copy-start | bytes 2359300
  116.5 5.0 %copy-start.4 = (bf16[1,8,16,3072]{3,2,1,0:T(8,128)(2,1)S(1)}, bf16[1,8,16,3072]{3,2,1,0:T(8,128)(2,1)}, u32[]{:S(2)}) copy-start(bf16[1,8,16,3072]{3,2,1,0:T(8,128)(2,1)} %param.4) | copy-start | bytes 2359300
  116.5 60.4 %all-to-all-start.2 = ((bf16[16,8,9216]{2,1,0:T(8,128)(2,1)}), bf16[16,8,9216]{2,1,0:T(8,128)(2,1)}, u32[]{:S(2)}, u32[]{:S(2)}) async-start(bf16[16,8,9216]{2,1,0:T(8,128)(2,1)} %get-tuple-element.24), calls=%async_computation.2 | async-start | bytes 4718592 | tf_op jit(solution)/shard_map/all_to_all | solution.py:329
  128.5 15.3 %collective-permute-start.2 = (bf16[2,48,3072]{2,1,0:T(8,128)(2,1)S(1)}, bf16[2,48,3072]{2,1,0:T(8,128)(2,1)S(1)}, u32[]{:S(2)}, u32[]{:S(2)}) collective-permute-start(bf16[2,48,3072]{2,1,0:T(8,128)(2,1)S(1)} %get-tuple-element.29), channel_id=1, source_target_pairs={{0,1},{1,2},{2,3},{3,4},{4,5},{5,6},{6,7},{7,8},{8,9},{9,10},{10,1... | collective-permute-start | bytes 1769480 | tf_op jit(solution)/shard_map/ppermute | solution.py:436
  130.5 15.0 %collective-permute-start.3 = (bf16[2,48,3072]{2,1,0:T(8,128)(2,1)S(1)}, bf16[2,48,3072]{2,1,0:T(8,128)(2,1)S(1)}, u32[]{:S(2)}, u32[]{:S(2)}) collective-permute-start(bf16[2,48,3072]{2,1,0:T(8,128)(2,1)S(1)} %get-tuple-element.30), channel_id=1, source_target_pairs={{1,0},{2,1},{3,2},{4,3},{5,4},{6,5},{7,6},{8,7},{9,8},{10,9},{11,1... | collective-permute-start | bytes 1769480 | tf_op jit(solution)/shard_map/ppermute | solution.py:435

commit v5 on v4

--- a/solution.py
+++ b/solution.py
@@ -146,12 +146,11 @@
     return left % spots == right % spots
 
 
-def temporal_scores_kernel(moved_ref, begun_ref, sent_ref, probs_ref, held, sems):
-    del begun_ref
+def temporal_scores_kernel(moved_ref, begun_ref, sent_ref, probs_ref, sem):
     frames, spots = moved_ref.shape[0], moved_ref.shape[1]
     channels = HEADS * HEAD_DIM
+    load = started(begun_ref, sent_ref.at[:, :, :channels], sem)
     same = same_position(frames * spots, spots)
-    stores = []
     for group in range(HEADS // TIME_HEADS):
         heads = range(group * TIME_HEADS, (group + 1) * TIME_HEADS)
         scores = [
@@ -165,17 +164,8 @@
         for part, head in zip(probs, heads):
             probs_ref[head] = part
         for part, head in zip(grads, heads):
-            held[:, :, lanes(head)] = chunked(part, frames).astype(BF16)
-        first, last = group * TIME_HEADS * HEAD_DIM, (group + 1) * TIME_HEADS * HEAD_DIM
-        stores.append(
-            started(
-                held.at[:, :, first:last],
-                sent_ref.at[:, :, channels + first : channels + last],
-                sems.at[group],
-            )
-        )
-    for store in stores:
-        store.wait()
+            sent_ref[:, :, lanes(HEADS + head)] = chunked(part, frames).astype(BF16)
+    load.wait()
 
 
 def temporal_grads_kernel(moved_ref, both_ref, probs_ref, out_ref, grad_ref, held, sems):
@@ -387,12 +377,12 @@
     moved = exchange(joined)
 
     own = rows_block(tokens, FWD_HEADS)
-    sent = call(
+    spatial = call(
         functools.partial(spatial_fwd_kernel, total_rows, breadth),
         HEADS // FWD_HEADS,
         [scalar, own, own, own, rims_block(FWD_HEADS), rims_block(FWD_HEADS)],
         chunk_block(FWD_HEADS, 0),
-        pltpu.HBM((parts, spots, 2 * channels), BF16),
+        pltpu.HBM((parts, spots, channels), BF16),
     )(first_row, query, key, value, low, high)
 
     moved = in_vmem(moved)
@@ -401,15 +391,14 @@
     sent, probs = pl.pallas_call(
         temporal_scores_kernel,
         in_specs=[in_place, anywhere],
-        out_specs=[anywhere, in_place],
-        out_shape=[pltpu.HBM(sent.shape, BF16), pltpu.VMEM((HEADS, tokens, tokens), F32)],
-        scratch_shapes=[
-            pltpu.VMEM((parts, spots, channels), BF16),
-            pltpu.SemaphoreType.DMA((groups,)),
+        out_specs=[in_place, in_place],
+        out_shape=[
+            pltpu.VMEM((parts, spots, 2 * channels), BF16),
+            pltpu.VMEM((HEADS, tokens, tokens), F32),
         ],
-        input_output_aliases={1: 0},
+        scratch_shapes=[pltpu.SemaphoreType.DMA],
         compiler_params=params,
-    )(moved, in_hbm(sent))
+    )(moved, in_hbm(spatial))
     both = in_vmem(exchange(sent))
 
     parts_out, spatial_grad = pl.pallas_call(

time: 181 us -> 180 us (level)
  no operation moved by 1% of the time
where the time goes in v5:
time: 180 us; the launch traced here: 179 us
  waiting for transfers between devices  73.8 us (41%)
  blocking collectives  44 us (24%)
  starting transfers between devices  30.5 us (17%)
  Pallas kernels  27.8 us (15%)
  local copies, waits for them, and re-layouts  2.28 us (1%)
    all_to_all x2, waiting for transfers between devices, exchange(): return lax.all_to_all(chunks, 'tm', split_axis=0, concat_axis=0, tiled=True)  54.6 us
    all_to_all x1, blocking collectives, exchange(): return lax.all_to_all(chunks, 'tm', split_axis=0, concat_axis=0, tiled=True)  44 us
    all_to_all x2, starting transfers between devices, exchange(): return lax.all_to_all(chunks, 'tm', split_axis=0, concat_axis=0, tiled=True)  14.6 us
    ppermute x1, waiting for transfers between devices, on_device(): low = lax.ppermute(to_high, 'rows', upward)  10.2 us
    ppermute x1, waiting for transfers between devices, on_device(): from_low = lax.ppermute(to_high, 'rows', upward)  7.38 us
    pallas_call x1, Pallas kernels, on_device(): call(functools.partial(spatial_bwd_kernel, total_rows, breadth), count, [...  6.98 us
    pallas_call x1, Pallas kernels, on_device(): call(functools.partial(spatial_fwd_kernel, total_rows, breadth), HEADS //...  6.15 us
    ppermute x1, starting transfers between devices, on_device(): high = lax.ppermute(to_low, 'rows', downward)  6.05 us
  transfers between devices with their start and end apart: 6, of which 5 were waited for; matrix products, arithmetic and copies ran while one was open for 0% of the time, Pallas kernels for 10%

profile of v5, /device:TPU:6, one launch (start us, length us, event | category | flops | bytes accessed | tf_op | source)
XLA Modules:
  0.0 179.0 jit_solution(11120418276748496379)
XLA Ops:
  0.6 2.7 %shard_map.75 = bf16[16,8,9216]{2,1,0:T(8,128)(2,1)} custom-call(bf16[16,8,3072]{2,1,0:T(8,128)(2,1)} %bitcast.20, bf16[16,8,3072]{2,1,0:T(8,128)(2,1)} %bitcast.11, bf16[16,8,3072]{2,1,0:T(8,128)(2,1)} %bitcast.23), custom_call_target="tpu_custom_call" | custom-call | tf_op jit(solution)/shard_map/pallas_call | solution.py:365
  3.4 9.6 %all-to-all-start = ((bf16[16,8,9216]{2,1,0:T(8,128)(2,1)}), bf16[16,8,9216]{2,1,0:T(8,128)(2,1)S(1)}, u32[]{:S(2)}, u32[]{:S(2)}) async-start(bf16[16,8,9216]{2,1,0:T(8,128)(2,1)} %shard_map.75), calls=%async_computation | async-start | bytes 4718592 | tf_op jit(solution)/shard_map/all_to_all | solution.py:319
  13.0 0.0 copy-start
  13.0 3.3 %shard_map.76 = (bf16[2,48,3072]{2,1,0:T(8,128)(2,1)}, bf16[2,48,3072]{2,1,0:T(8,128)(2,1)}) custom-call(bf16[128,3072]{1,0:T(8,128)(2,1)} %bitcast.12, bf16[128,3072]{1,0:T(8,128)(2,1)} %bitcast.16, bf16[128,3072]{1,0:T(8,128)(2,1)} %bitcast.13, bf16[128,3072]{1,0:T(8,128)(2,1)} %bitcast.17), custom_call_target="tpu_custom_call" | custom-call | tf_op jit(solution)/shard_map/pallas_call | solution.py:354
  16.3 1.9 %collective-permute-start = (bf16[2,48,3072]{2,1,0:T(8,128)(2,1)}, bf16[2,48,3072]{2,1,0:T(8,128)(2,1)}, u32[]{:S(2)}, u32[]{:S(2)}) collective-permute-start(bf16[2,48,3072]{2,1,0:T(8,128)(2,1)} %get-tuple-element.20), channel_id=1, source_target_pairs={{0,1},{1,2},{2,3},{3,4},{4,5},{5,6},{6,7},{7,8},{8,9},{9,10},{10,1... | collective-permute-start | bytes 1769480 | tf_op jit(solution)/shard_map/ppermute | solution.py:361
  18.2 6.0 %collective-permute-start.1 = (bf16[2,48,3072]{2,1,0:T(8,128)(2,1)}, bf16[2,48,3072]{2,1,0:T(8,128)(2,1)}, u32[]{:S(2)}, u32[]{:S(2)}) collective-permute-start(bf16[2,48,3072]{2,1,0:T(8,128)(2,1)} %get-tuple-element.21), channel_id=1, source_target_pairs={{1,0},{2,1},{3,2},{4,3},{5,4},{6,5},{7,6},{8,7},{9,8},{10,9},{11,1... | collective-permute-start | bytes 1769480 | tf_op jit(solution)/shard_map/ppermute | solution.py:362
  24.2 10.2 %collective-permute-done.low_ref = bf16[2,48,3072]{2,1,0:T(8,128)(2,1)} collective-permute-done((bf16[2,48,3072]{2,1,0:T(8,128)(2,1)}, bf16[2,48,3072]{2,1,0:T(8,128)(2,1)}, u32[]{:S(2)}, u32[]{:S(2)}) %collective-permute-start) | collective-permute-done | bytes 589856 | tf_op jit(solution)/shard_map/ppermute | solution.py:361
  34.5 0.0 collective-permute-done.1.high_ref
  34.5 0.0 copy-done
  34.5 0.0 copy-start.1
  34.5 1.1 copy-done.1
  35.6 0.0 copy-start.3
  35.6 1.1 copy-done.3
  36.7 6.1 %shard_map.77.begun_ref = bf16[16,8,3072]{2,1,0:T(8,128)(2,1)} custom-call(s32[1]{0:T(128)} %bitcast.3.first_ref, bf16[128,3072]{1,0:T(8,128)(2,1)S(1)} %bitcast.21, bf16[128,3072]{1,0:T(8,128)(2,1)S(1)} %bitcast.14, bf16[128,3072]{1,0:T(8,128)(2,1)S(1)} %bitcast.18, bf16[2,48,3072]{2,1,0:T(8,128)(2,1)} %collective-permute-done.low_ref, ...), custom_call_target="tpu_custom_call" | custom-call | tf_op jit(solution)/shard_map/pallas_call | solution.py:380
  42.9 25.1 %all-to-all-done.moved_ref = bf16[16,8,9216]{2,1,0:T(8,128)(2,1)S(1)} async-done(((bf16[16,8,9216]{2,1,0:T(8,128)(2,1)}), bf16[16,8,9216]{2,1,0:T(8,128)(2,1)S(1)}, u32[]{:S(2)}, u32[]{:S(2)}) %all-to-all-start) | async-done | bytes 2359328 | tf_op jit(solution)/shard_map/all_to_all | solution.py:319
  67.9 1.3 shard_map.78
  69.2 44.0 %all_to_all.15.both_ref = bf16[16,8,6144]{2,1,0:T(8,128)(2,1)S(1)} all-to-all(bf16[16,8,6144]{2,1,0:T(8,128)(2,1)S(1)} %get-tuple-element.22), channel_id=1, replica_groups=mesh['tm'=16,'rows'=16] {'tm'}, dimensions={0} | all-to-all | bytes 3145728 | tf_op jit(solution)/shard_map/all_to_all | solution.py:319
  113.2 2.3 %shard_map.79 = (bf16[16,8,9216]{2,1,0:T(8,128)(2,1)}, bf16[16,8,3072]{2,1,0:T(8,128)(2,1)}) custom-call(bf16[16,8,9216]{2,1,0:T(8,128)(2,1)S(1)} %all-to-all-done.moved_ref, bf16[16,8,6144]{2,1,0:T(8,128)(2,1)S(1)} %all_to_all.15.both_ref, f32[24,128,128]{2,1,0:T(8,128)S(1)} %get-tuple-element.23.probs_ref), custom_call_target="tpu_custom_call" | custom-call | tf_op jit(solution)/shard_map/pallas_call | solution.py:404
  115.5 0.0 copy-start.2
  115.5 0.0 copy-start.4
  115.5 5.0 %all-to-all-start.2 = ((bf16[16,8,9216]{2,1,0:T(8,128)(2,1)}), bf16[16,8,9216]{2,1,0:T(8,128)(2,1)}, u32[]{:S(2)}, u32[]{:S(2)}) async-start(bf16[16,8,9216]{2,1,0:T(8,128)(2,1)} %get-tuple-element.24), calls=%async_computation.2 | async-start | bytes 4718592 | tf_op jit(solution)/shard_map/all_to_all | solution.py:319
  120.5 0.0 copy-done.2
  120.6 0.0 copy-done.4
  120.6 7.0 %shard_map.80 = (bf16[16,8,3072]{2,1,0:T(8,128)(2,1)}, f32[128,3072]{1,0:T(8,128)S(1)}, f32[128,3072]{1,0:T(8,128)S(1)}, bf16[2,48,3072]{2,1,0:T(8,128)(2,1)S(1)}, bf16[2,48,3072]{2,1,0:T(8,128)(2,1)S(1)}) custom-call(s32[1]{0:T(128)} %bitcast.3.first_ref, bf16[128,3072]{1,0:T(8,128)(2,1)S(1)} %bitcast.22, bf16[128,3072]{1,0:T(8,128)(2,1)S(1)} %bitcast.15, ...), custom_call_target="tpu_custom_call" | custom-call | tf_op jit(solution)/shard_map/pallas_call | solution.py:417
  127.5 1.9 %collective-permute-start.2 = (bf16[2,48,3072]{2,1,0:T(8,128)(2,1)S(1)}, bf16[2,48,3072]{2,1,0:T(8,128)(2,1)S(1)}, u32[]{:S(2)}, u32[]{:S(2)}) collective-permute-start(bf16[2,48,3072]{2,1,0:T(8,128)(2,1)S(1)} %get-tuple-element.29), channel_id=1, source_target_pairs={{0,1},{1,2},{2,3},{3,4},{4,5},{5,6},{6,7},{7,8},{8,9},{9,10},{10,1... | collective-permute-start | bytes 1769480 | tf_op jit(solution)/shard_map/ppermute | solution.py:425
  129.5 6.0 %collective-permute-start.3 = (bf16[2,48,3072]{2,1,0:T(8,128)(2,1)S(1)}, bf16[2,48,3072]{2,1,0:T(8,128)(2,1)S(1)}, u32[]{:S(2)}, u32[]{:S(2)}) collective-permute-start(bf16[2,48,3072]{2,1,0:T(8,128)(2,1)S(1)} %get-tuple-element.30), channel_id=1, source_target_pairs={{1,0},{2,1},{3,2},{4,3},{5,4},{6,5},{7,6},{8,7},{9,8},{10,9},{11,1... | collective-permute-start | bytes 1769480 | tf_op jit(solution)/shard_map/ppermute | solution.py:424
  135.5 7.4 %collective-permute-done.2.from_low_ref = bf16[2,48,3072]{2,1,0:T(8,128)(2,1)S(1)} collective-permute-done((bf16[2,48,3072]{2,1,0:T(8,128)(2,1)S(1)}, bf16[2,48,3072]{2,1,0:T(8,128)(2,1)S(1)}, u32[]{:S(2)}, u32[]{:S(2)}) %collective-permute-start.2) | collective-permute-done | bytes 589856 | tf_op jit(solution)/shard_map/ppermute | solution.py:425
  142.9 1.5 collective-permute-done.3.from_high_ref
  144.4 1.9 %shard_map.81 = (bf16[16,8,3072]{2,1,0:T(8,128)(2,1)}, bf16[128,3072]{1,0:T(8,128)(2,1)}) custom-call(f32[128,3072]{1,0:T(8,128)S(1)} %get-tuple-element.27.ks_ref, f32[128,3072]{1,0:T(8,128)S(1)} %get-tuple-element.28.vs_ref, bf16[2,48,3072]{2,1,0:T(8,128)(2,1)S(1)} %collective-permute-done.2.from_low_ref, ...), custom_call_target="tpu_custom_call" | custom-call | tf_op jit(solution)/shard_map/pallas_call | solution.py:428
  146.4 29.6 %all-to-all-done.2.back_ref = bf16[16,8,9216]{2,1,0:T(8,128)(2,1)} async-done(((bf16[16,8,9216]{2,1,0:T(8,128)(2,1)}), bf16[16,8,9216]{2,1,0:T(8,128)(2,1)}, u32[]{:S(2)}, u32[]{:S(2)}) %all-to-all-start.2) | async-done | bytes 2359328 | tf_op jit(solution)/shard_map/all_to_all | solution.py:319
  175.9 3.1 %shard_map.82 = (bf16[16,8,3072]{2,1,0:T(8,128)(2,1)}, bf16[16,8,3072]{2,1,0:T(8,128)(2,1)}, bf16[16,8,3072]{2,1,0:T(8,128)(2,1)}) custom-call(bf16[16,8,9216]{2,1,0:T(8,128)(2,1)} %all-to-all-done.2.back_ref, bf16[16,8,3072]{2,1,0:T(8,128)(2,1)} %get-tuple-element.26.qs_ref, bf16[16,8,3072]{2,1,0:T(8,128)(2,1)} %get-tuple-element.31.ks_ref), custom_call_target="tpu_custom_call" | custom-call | tf_op jit(solution)/shard_map/pallas_call | solution.py:436
Async XLA Ops:
  3.4 64.6 %all-to-all-start = ((bf16[16,8,9216]{2,1,0:T(8,128)(2,1)}), bf16[16,8,9216]{2,1,0:T(8,128)(2,1)S(1)}, u32[]{:S(2)}, u32[]{:S(2)}) async-start(bf16[16,8,9216]{2,1,0:T(8,128)(2,1)} %shard_map.75), calls=%async_computation | async-start | bytes 4718592 | tf_op jit(solution)/shard_map/all_to_all | solution.py:319
  13.0 21.5 %copy-start = (bf16[1,8,16,3072]{3,2,1,0:T(8,128)(2,1)S(1)}, bf16[1,8,16,3072]{3,2,1,0:T(8,128)(2,1)}, u32[]{:S(2)}) copy-start(bf16[1,8,16,3072]{3,2,1,0:T(8,128)(2,1)} %param.5) | copy-start | bytes 2359300
  16.3 18.2 %collective-permute-start = (bf16[2,48,3072]{2,1,0:T(8,128)(2,1)}, bf16[2,48,3072]{2,1,0:T(8,128)(2,1)}, u32[]{:S(2)}, u32[]{:S(2)}) collective-permute-start(bf16[2,48,3072]{2,1,0:T(8,128)(2,1)} %get-tuple-element.20), channel_id=1, source_target_pairs={{0,1},{1,2},{2,3},{3,4},{4,5},{5,6},{6,7},{7,8},{8,9},{9,10},{10,1... | collective-permute-start | bytes 1769480 | tf_op jit(solution)/shard_map/ppermute | solution.py:361
  18.2 16.3 %collective-permute-start.1 = (bf16[2,48,3072]{2,1,0:T(8,128)(2,1)}, bf16[2,48,3072]{2,1,0:T(8,128)(2,1)}, u32[]{:S(2)}, u32[]{:S(2)}) collective-permute-start(bf16[2,48,3072]{2,1,0:T(8,128)(2,1)} %get-tuple-element.21), channel_id=1, source_target_pairs={{1,0},{2,1},{3,2},{4,3},{5,4},{6,5},{7,6},{8,7},{9,8},{10,9},{11,1... | collective-permute-start | bytes 1769480 | tf_op jit(solution)/shard_map/ppermute | solution.py:362
  34.5 1.1 copy-start.1
  35.6 1.1 copy-start.3
  115.5 5.0 %copy-start.2 = (bf16[1,8,16,3072]{3,2,1,0:T(8,128)(2,1)S(1)}, bf16[1,8,16,3072]{3,2,1,0:T(8,128)(2,1)}, u32[]{:S(2)}) copy-start(bf16[1,8,16,3072]{3,2,1,0:T(8,128)(2,1)} %param.6) | copy-start | bytes 2359300
  115.5 5.0 %copy-start.4 = (bf16[1,8,16,3072]{3,2,1,0:T(8,128)(2,1)S(1)}, bf16[1,8,16,3072]{3,2,1,0:T(8,128)(2,1)}, u32[]{:S(2)}) copy-start(bf16[1,8,16,3072]{3,2,1,0:T(8,128)(2,1)} %param.4) | copy-start | bytes 2359300
  115.5 60.4 %all-to-all-start.2 = ((bf16[16,8,9216]{2,1,0:T(8,128)(2,1)}), bf16[16,8,9216]{2,1,0:T(8,128)(2,1)}, u32[]{:S(2)}, u32[]{:S(2)}) async-start(bf16[16,8,9216]{2,1,0:T(8,128)(2,1)} %get-tuple-element.24), calls=%async_computation.2 | async-start | bytes 4718592 | tf_op jit(solution)/shard_map/all_to_all | solution.py:319
  127.5 15.4 %collective-permute-start.2 = (bf16[2,48,3072]{2,1,0:T(8,128)(2,1)S(1)}, bf16[2,48,3072]{2,1,0:T(8,128)(2,1)S(1)}, u32[]{:S(2)}, u32[]{:S(2)}) collective-permute-start(bf16[2,48,3072]{2,1,0:T(8,128)(2,1)S(1)} %get-tuple-element.29), channel_id=1, source_target_pairs={{0,1},{1,2},{2,3},{3,4},{4,5},{5,6},{6,7},{7,8},{8,9},{9,10},{10,1... | collective-permute-start | bytes 1769480 | tf_op jit(solution)/shard_map/ppermute | solution.py:425
  129.5 15.0 %collective-permute-start.3 = (bf16[2,48,3072]{2,1,0:T(8,128)(2,1)S(1)}, bf16[2,48,3072]{2,1,0:T(8,128)(2,1)S(1)}, u32[]{:S(2)}, u32[]{:S(2)}) collective-permute-start(bf16[2,48,3072]{2,1,0:T(8,128)(2,1)S(1)} %get-tuple-element.30), channel_id=1, source_target_pairs={{1,0},{2,1},{3,2},{4,3},{5,4},{6,5},{7,6},{8,7},{9,8},{10,9},{11,1... | collective-permute-start | bytes 1769480 | tf_op jit(solution)/shard_map/ppermute | solution.py:424
